TPU v7x, 32 devices: a whole 2x2x4 slice. The times are simulated.
32 devices in a mesh: groups: 2 (over x), rows: 4 (over y, core), cols: 4 (over z).
Axes of the slice: x: 2, y: 2, z: 4, core: 2. Of those that a mesh axis runs over, the one named last changes fastest.
Arguments:
- points: float32 [24, 13312], P(None, ('groups', 'rows', 'cols')), parts along dimension 1, may hold values from -6 to 6
- lengthscale: float32 [48], P('groups'), parts along dimension 0, may hold values from 1.5 to 6
- target: float32 [13312], P(('groups', 'rows', 'cols')), parts along dimension 0, may hold values from -6 to 6
- probes: int32 [7, 13312], P(None, ('groups', 'rows', 'cols')), parts along dimension 1, may hold values from 0 to 1
- noise: float32 [13312], P(('groups', 'rows', 'cols')), parts along dimension 0, may hold values from 0.05 to 0.5
Outputs:
- product: float32 [8, 13312], P(None, ('groups', 'rows', 'cols')), parts along dimension 1
There are 2 independent parts, one for each index of `groups`. A program takes and returns all parts, laid end to end along the dimension named above; each array names one. Nothing has to cross between parts.
All inputs are finite; a program needn't handle non-finite values.
Results may differ from a plain program's by a relative error of at most 0.0085.
Values may be sent and summed in bfloat16 or wider, within the bound.
No kernel may reach another device: no remote copies, remote signals or barrier semaphores. Data moves between devices by JAX's collectives and lax.ppermute only.
A program may use at most 64 MiB of HBM per device.

v0:
```python
import jax
import jax.numpy as jnp
from jax import lax
from jax.sharding import PartitionSpec as P


def add_tile(row_scaled, row_norm, piece):
    col_scaled, col_vectors = piece
    col_norm = jnp.sum(col_scaled.astype(jnp.float32) ** 2, axis=0)
    cross = lax.dot_general(
        col_scaled, row_scaled, (((0,), (0,)), ((), ())), preferred_element_type=jnp.float32
    )
    dist = col_norm[:, None] + row_norm[None, :] - 2.0 * cross
    kernel = jnp.exp(-0.5 * dist).astype(jnp.bfloat16)
    return jnp.dot(col_vectors, kernel, preferred_element_type=jnp.float32)


def local(points, lengthscale, target, probes, noise):
    scaled = (points / lengthscale[:, None]).astype(jnp.bfloat16)
    signs = (2 * probes - 1).astype(jnp.float32)
    vectors = jnp.concatenate([target[None, :], signs], axis=0).astype(jnp.bfloat16)
    own_norm = jnp.sum(scaled.astype(jnp.float32) ** 2, axis=0)
    mine = add_tile(
        scaled,
        own_norm,
        (
            lax.all_gather(scaled, ("rows", "cols"), axis=1, tiled=True),
            lax.all_gather(vectors, ("rows", "cols"), axis=1, tiled=True),
        ),
    )
    return mine + noise[None, :] * vectors.astype(jnp.float32)


def solution(mesh):
    return jax.shard_map(
        local,
        mesh=mesh,
        in_specs=(
            P(None, ("groups", "rows", "cols")),
            P("groups"),
            P(("groups", "rows", "cols")),
            P(None, ("groups", "rows", "cols")),
            P(("groups", "rows", "cols")),
        ),
        out_specs=P(None, ("groups", "rows", "cols")),
        check_vma=False,
    )
```

profile of v0, /device:TPU:0, one launch (start us, length us, event | category | flops | bytes accessed | tf_op | source)
XLA Modules:
  0.0 73.1 jit_solution(17297565393656126259)
XLA Ops:
  0.0 0.9 %multiply_reduce_fusion.1 = (f32[416]{0:T(512)S(1)}, bf16[24,416]{1,0:T(8,128)(2,1)S(1)}) fusion(f32[24,416]{1,0:T(8,128)} %param.5, f32[24]{0:T(128)} %param.6), kind=kLoop, calls=%fused_computation.4 | loop fusion | flops 49504 | bytes 61664 | tf_op jit(solution)/shard_map/reduce_sum | solution.py:22
  0.9 37.5 %all-gather.1 = bf16[16,416,24]{1,2,0:T(8,128)(2,1)S(1)} all-gather(bf16[1,416,24]{1,2,0:T(8,128)(2,1)S(1)} %bitcast.14), channel_id=1, replica_groups=mesh['groups'=2,'rows'=4,'cols'=4] {'rows','cols'}, dimensions={0}, use_global_device_ids=true | all-gather | bytes 339456 | tf_op jit(solution)/shard_map/all_gather | solution.py:27
  38.4 0.1 copy.9
  38.5 0.0 copy-start
  38.5 0.0 copy-start.1
  38.5 0.5 reshape.7
  39.0 0.1 multiply_reduce_fusion
  39.1 0.1 copy-done
  39.2 0.0 copy-start.2
  39.2 0.0 copy-done.1
  39.3 29.5 %all-gather = bf16[16,416,8]{1,2,0:T(8,128)(2,1)S(1)} all-gather(bf16[1,416,8]{1,2,0:T(8,128)(2,1)S(1)} %fusion.2), channel_id=1, replica_groups=mesh['groups'=2,'rows'=4,'cols'=4] {'rows','cols'}, dimensions={0}, use_global_device_ids=true | all-gather | bytes 113152 | tf_op jit(solution)/shard_map/all_gather | solution.py:28
  68.8 0.2 reshape.5
  69.0 0.0 copy-done.2
  69.0 4.1 %fusion.1 = f32[8,416]{1,0:T(8,128)} fusion(bf16[6656,8]{0,1:T(8,128)(2,1)S(1)} %reshape.5, bf16[6656,24]{0,1:T(8,128)(2,1)S(1)} %reshape.7, bf16[24,416]{1,0:T(8,128)(2,1)S(1)} %get-tuple-element.6, f32[416]{0:T(512)S(1)} %get-tuple-element.5, f32[6656]{0:T(1024)S(1)} %multiply_reduce_fusion, f32[416]{0:T(512)S(1)} %copy-done.2, ...), kind=kOutput, calls=%fused_computation.2 | convolution fusion | flops 191073792 | bytes 495872 | tf_op jit(solution)/shard_map/dot_general | solution.py:15
  (5 shorter events, 0.1 us)
Async XLA Ops:
  38.5 0.7 copy-start
  38.5 0.7 copy-start.1
  39.2 29.8 %copy-start.2 = (f32[416]{0:T(512)S(1)}, f32[416]{0:T(512)}, u32[]{:S(2)}) copy-start(f32[416]{0:T(512)} %param.9) | copy-start | bytes 4996
where the time goes:
time: 73.3 us; the launch traced here: 73.1 us
  blocking collectives  67 us (91%)
  matrix products  4.06 us (6%)
  other arithmetic  1.02 us (1%)
  local copies, waits for them, and re-layouts  0.93 us (1%)
    all_gather x1, blocking collectives, local(): lax.all_gather(scaled, ('rows', 'cols'), axis=1, tiled=True)  37.5 us
    all_gather x1, blocking collectives, local(): lax.all_gather(vectors, ('rows', 'cols'), axis=1, tiled=True)  29.5 us
    dot_general x1, matrix products, add_tile(): return jnp.dot(col_vectors, kernel, preferred_element_type=jnp.float32)  4.06 us

commit v1 on v0

v1 whole, which is shorter than its diff:
```python
import functools

import jax
import jax.numpy as jnp
from jax import lax
from jax.experimental import pallas as pl
from jax.experimental.pallas import tpu as pltpu
from jax.sharding import PartitionSpec as P

VMEM = pltpu.VMEM
IN_VMEM = pl.BlockSpec(memory_space=VMEM)


def near(x):
    return pltpu.with_memory_space_constraint(x, VMEM)


def prepare_kernel(points_ref, lengthscale_ref, target_ref, probes_ref, block_ref):
    features = points_ref.shape[0]
    wide = jnp.broadcast_to(lengthscale_ref[...], (features, features))
    row = lax.broadcasted_iota(jnp.int32, wide.shape, 0)
    col = lax.broadcasted_iota(jnp.int32, wide.shape, 1)
    scale = jnp.sum(jnp.where(row == col, wide, 0.0), axis=1, keepdims=True)
    scaled = points_ref[...] / scale
    signs = (2 * probes_ref[...] - 1).astype(jnp.float32)
    block = jnp.concatenate([scaled, target_ref[...], signs], axis=0)
    block_ref[...] = block.astype(jnp.bfloat16)


def augmented(block, features, own):
    x = block.astype(jnp.float32)
    row = lax.broadcasted_iota(jnp.int32, x.shape, 0)
    x = jnp.where(row < features, x, 0.0)
    half = -0.5 * jnp.sum(x * x, axis=0, keepdims=True)
    high = half.astype(jnp.bfloat16).astype(jnp.float32)
    rest = half - high
    middle = rest.astype(jnp.bfloat16).astype(jnp.float32)
    parts = [high, middle, rest - middle]
    rows = [1.0, 1.0, 1.0] + parts if own else parts + [1.0, 1.0, 1.0]
    for place, value in enumerate(rows):
        x = jnp.where(row == features + place, value, x)
    return x.astype(jnp.bfloat16)


def add_blocks(features, counts, last, *refs):
    piece_refs, rest = refs[: len(counts)], refs[len(counts) :]
    own_ref, rest = rest[0], rest[1:]
    noise_ref, rest = (rest[0], rest[1:]) if last else (None, rest)
    sum_ref, out_ref = rest if len(rest) == 2 else (None, rest[0])
    own = own_ref[...]
    own_side = augmented(own, features, True)
    blocks = [(ref, k) for ref, count in zip(piece_refs, counts) for k in range(count)]
    low = features // 16 * 16

    def exponent(ref, k):
        return lax.dot_general(
            augmented(ref[k], features, False),
            own_side,
            (((0,), (0,)), ((), ())),
            preferred_element_type=jnp.float32,
        )

    total = None
    ahead = exponent(*blocks[0])
    for at, (ref, k) in enumerate(blocks):
        now = ahead
        if at + 1 < len(blocks):
            ahead = exponent(*blocks[at + 1])
        kernel = jnp.exp(now).astype(jnp.bfloat16)
        term = jnp.dot(ref[k][low:], kernel, preferred_element_type=jnp.float32)
        total = term if total is None else total + term
    total = total[features - low :]
    if sum_ref is not None:
        total = total + sum_ref[...]
    if last:
        total = total + noise_ref[...] * own[features:].astype(jnp.float32)
    out_ref[...] = total


def add(features, pieces, own, noise=None, total=None):
    rows, width = own.shape
    counts = tuple(piece.shape[0] for piece in pieces)
    last = noise is not None
    operands = [near(piece) for piece in pieces] + [near(own)]
    if last:
        operands.append(noise)
    if total is not None:
        operands.append(near(total))
    shape = (rows - features, width)
    out = jax.ShapeDtypeStruct(shape, jnp.float32) if last else VMEM(shape, jnp.float32)
    work = sum(counts) * width * width
    return pl.pallas_call(
        functools.partial(add_blocks, features, counts, last),
        out_shape=out,
        in_specs=[IN_VMEM] * len(operands),
        out_specs=IN_VMEM,
        cost_estimate=pl.CostEstimate(flops=2 * work * 512, bytes_accessed=0, transcendentals=work),
    )(*operands)


def swap(x, mesh_shape, row_bits, col_bits):
    rows, cols = mesh_shape
    pairs = [
        (r * cols + c, (r ^ row_bits) * cols + (c ^ col_bits)) for r in range(rows) for c in range(cols)
    ]
    return lax.ppermute(x, ("rows", "cols"), pairs)


def powers(top):
    found = []
    while top > 1:
        top //= 2
        found.append(top)
    return found


def local(mesh_shape, points, lengthscale, target, probes, noise):
    features, width = points.shape
    rows, cols = mesh_shape
    vectors = probes.shape[0] + 1
    block = pl.pallas_call(
        prepare_kernel,
        out_shape=VMEM((features + vectors, width), jnp.bfloat16),
        in_specs=[IN_VMEM] * 4,
        out_specs=IN_VMEM,
    )(points, lengthscale[None, :], target[None, :], probes)
    mine = block[None]
    for bits in powers(cols):
        mine = jnp.concatenate([mine, swap(mine, mesh_shape, 1, bits)], axis=0)
    for bits in powers(rows)[:-1]:
        mine = jnp.concatenate([mine, swap(mine, mesh_shape, bits + 1, 0)], axis=0)
    other = swap(mine, mesh_shape, 1, 0)
    total = add(features, [mine], block)
    return add(features, [other], block, noise[None, :], total)


def solution(mesh):
    mesh_shape = (mesh.shape["rows"], mesh.shape["cols"])
    return jax.shard_map(
        functools.partial(local, mesh_shape),
        mesh=mesh,
        in_specs=(
            P(None, ("groups", "rows", "cols")),
            P("groups"),
            P(("groups", "rows", "cols")),
            P(None, ("groups", "rows", "cols")),
            P(("groups", "rows", "cols")),
        ),
        out_specs=P(None, ("groups", "rows", "cols")),
        check_vma=False,
    )
```

time: 73.3 us -> 21.4 us (0.29)
  the two profiles are of different devices: /device:TPU:0 before, /device:TPU:25 now
where the time goes in v1:
time: 21.4 us; the launch traced here: 21.2 us
  waiting for transfers between devices  12.9 us (60%)
  Pallas kernels  5.37 us (25%)
  starting transfers between devices  2.8 us (13%)
    ppermute x4, waiting for transfers between devices, swap(): return lax.ppermute(x, ('rows', 'cols'), pairs)  12.9 us
    pallas_call x2, Pallas kernels, add(): pl.pallas_call(functools.partial(add_blocks, features, counts, last), out...  4.47 us
    ppermute x4, starting transfers between devices, swap(): return lax.ppermute(x, ('rows', 'cols'), pairs)  2.8 us
    pallas_call x1, Pallas kernels, local(): pl.pallas_call(prepare_kernel, out_shape=VMEM((features + vectors, width)...  0.9 us
  transfers between devices with their start and end apart: 4, of which 3 were waited for; matrix products, arithmetic and copies ran while one was open for 0% of the time, Pallas kernels for 7%

profile of v1, /device:TPU:25, one launch (start us, length us, event | category | flops | bytes accessed | tf_op | source)
XLA Modules:
  0.0 21.2 jit_solution(11319601565491070430)
XLA Ops:
  0.0 0.9 %shard_map.55.refs_1_ = bf16[32,416]{1,0:T(8,128)(2,1)S(1)} custom-call(f32[24,416]{1,0:T(8,128)} %points_ref.1, f32[1,24]{1,0:T(1,128)} %bitcast.9, f32[1,416]{1,0:T(1,128)} %bitcast.8, s32[7,416]{1,0:T(8,128)} %probes_ref.1), custom_call_target="tpu_custom_call" | custom-call | tf_op jit(solution)/shard_map/pallas_call | solution.py:121
  0.9 0.7 %collective-permute-start = (bf16[1,32,416]{2,1,0:T(8,128)(2,1)S(1)}, bf16[1,32,416]{2,1,0:T(8,128)(2,1)S(1)}, u32[]{:S(2)}, u32[]{:S(2)}) collective-permute-start(bf16[1,32,416]{2,1,0:T(8,128)(2,1)S(1)} %bitcast.4), channel_id=1, source_target_pairs={{0,6},{1,7},{2,4},{3,5},{4,2},{5,3},{6,0},{7,1},{8,14},{9,15},{10,... | collective-permute-start | bytes 79880 | tf_op jit(solution)/shard_map/ppermute | solution.py:106
  1.6 4.8 %collective-permute-done = bf16[1,32,416]{2,1,0:T(8,128)(2,1)S(1)} collective-permute-done((bf16[1,32,416]{2,1,0:T(8,128)(2,1)S(1)}, bf16[1,32,416]{2,1,0:T(8,128)(2,1)S(1)}, u32[]{:S(2)}, u32[]{:S(2)}) %collective-permute-start) | collective-permute-done | bytes 26656 | tf_op jit(solution)/shard_map/ppermute | solution.py:106
  6.4 0.1 collective-permute-start.1
  6.5 4.1 %collective-permute-done.1 = bf16[2,32,416]{2,1,0:T(8,128)(2,1)S(1)} collective-permute-done((bf16[2,32,416]{2,1,0:T(8,128)(2,1)S(1)}, bf16[2,32,416]{2,1,0:T(8,128)(2,1)S(1)}, u32[]{:S(2)}, u32[]{:S(2)}) %collective-permute-start.1) | collective-permute-done | bytes 53280 | tf_op jit(solution)/shard_map/ppermute | solution.py:106
  10.6 1.6 %collective-permute-start.2 = (bf16[4,32,416]{2,1,0:T(8,128)(2,1)S(1)}, bf16[4,32,416]{2,1,0:T(8,128)(2,1)S(1)}, u32[]{:S(2)}, u32[]{:S(2)}) collective-permute-start(bf16[4,32,416]{2,1,0:T(8,128)(2,1)S(1)} %pad_maximum_fusion.1), channel_id=1, source_target_pairs={{0,12},{1,13},{2,14},{3,15},{4,8},{5,9},{6,10},{7,11},{8,4},{9,5},... | collective-permute-start | bytes 319496 | tf_op jit(solution)/shard_map/ppermute | solution.py:106
  12.2 4.0 %collective-permute-done.2 = bf16[4,32,416]{2,1,0:T(8,128)(2,1)S(1)} collective-permute-done((bf16[4,32,416]{2,1,0:T(8,128)(2,1)S(1)}, bf16[4,32,416]{2,1,0:T(8,128)(2,1)S(1)}, u32[]{:S(2)}, u32[]{:S(2)}) %collective-permute-start.2) | collective-permute-done | bytes 106528 | tf_op jit(solution)/shard_map/ppermute | solution.py:106
  16.3 0.5 %collective-permute-start.3 = (bf16[8,32,416]{2,1,0:T(8,128)(2,1)S(1)}, bf16[8,32,416]{2,1,0:T(8,128)(2,1)S(1)}, u32[]{:S(2)}, u32[]{:S(2)}) collective-permute-start(bf16[8,32,416]{2,1,0:T(8,128)(2,1)S(1)} %pad_maximum_fusion.refs_0_), channel_id=1, source_target_pairs={{0,4},{1,5},{2,6},{3,7},{4,0},{5,1},{6,2},{7,3},{8,12},{9,13},{10,... | collective-permute-start | bytes 638984 | tf_op jit(solution)/shard_map/ppermute | solution.py:106
  16.7 1.5 %shard_map.56.refs_3_ = f32[8,416]{1,0:T(8,128)S(1)} custom-call(bf16[8,32,416]{2,1,0:T(8,128)(2,1)S(1)} %pad_maximum_fusion.refs_0_, bf16[32,416]{1,0:T(8,128)(2,1)S(1)} %shard_map.55.refs_1_), custom_call_target="tpu_custom_call" | custom-call | flops 1417674752 | tf_op jit(solution)/shard_map/pallas_call | solution.py:92
  18.2 0.0 collective-permute-done.3.refs_0_
  18.2 3.0 %shard_map.57 = f32[8,416]{1,0:T(8,128)} custom-call(bf16[8,32,416]{2,1,0:T(8,128)(2,1)S(1)} %collective-permute-done.3.refs_0_, bf16[32,416]{1,0:T(8,128)(2,1)S(1)} %shard_map.55.refs_1_, f32[1,416]{1,0:T(1,128)} %bitcast.10, f32[8,416]{1,0:T(8,128)S(1)} %shard_map.56.refs_3_), custom_call_target="tpu_custom_call" | custom-call | flops 1417674752 | tf_op jit(solution)/shard_map/pallas_call | solution.py:92
  (3 shorter events, 0.1 us)
Async XLA Ops:
  0.9 5.5 %collective-permute-start = (bf16[1,32,416]{2,1,0:T(8,128)(2,1)S(1)}, bf16[1,32,416]{2,1,0:T(8,128)(2,1)S(1)}, u32[]{:S(2)}, u32[]{:S(2)}) collective-permute-start(bf16[1,32,416]{2,1,0:T(8,128)(2,1)S(1)} %bitcast.4), channel_id=1, source_target_pairs={{0,6},{1,7},{2,4},{3,5},{4,2},{5,3},{6,0},{7,1},{8,14},{9,15},{10,... | collective-permute-start | bytes 79880 | tf_op jit(solution)/shard_map/ppermute | solution.py:106
  6.4 4.2 %collective-permute-start.1 = (bf16[2,32,416]{2,1,0:T(8,128)(2,1)S(1)}, bf16[2,32,416]{2,1,0:T(8,128)(2,1)S(1)}, u32[]{:S(2)}, u32[]{:S(2)}) collective-permute-start(bf16[2,32,416]{2,1,0:T(8,128)(2,1)S(1)} %pad_maximum_fusion.2), channel_id=1, source_target_pairs={{0,5},{1,4},{2,7},{3,6},{4,1},{5,0},{6,3},{7,2},{8,13},{9,12},{10,... | collective-permute-start | bytes 159752 | tf_op jit(solution)/shard_map/ppermute | solution.py:106
  10.6 5.6 %collective-permute-start.2 = (bf16[4,32,416]{2,1,0:T(8,128)(2,1)S(1)}, bf16[4,32,416]{2,1,0:T(8,128)(2,1)S(1)}, u32[]{:S(2)}, u32[]{:S(2)}) collective-permute-start(bf16[4,32,416]{2,1,0:T(8,128)(2,1)S(1)} %pad_maximum_fusion.1), channel_id=1, source_target_pairs={{0,12},{1,13},{2,14},{3,15},{4,8},{5,9},{6,10},{7,11},{8,4},{9,5},... | collective-permute-start | bytes 319496 | tf_op jit(solution)/shard_map/ppermute | solution.py:106
  16.3 1.9 %collective-permute-start.3 = (bf16[8,32,416]{2,1,0:T(8,128)(2,1)S(1)}, bf16[8,32,416]{2,1,0:T(8,128)(2,1)S(1)}, u32[]{:S(2)}, u32[]{:S(2)}) collective-permute-start(bf16[8,32,416]{2,1,0:T(8,128)(2,1)S(1)} %pad_maximum_fusion.refs_0_), channel_id=1, source_target_pairs={{0,4},{1,5},{2,6},{3,7},{4,0},{5,1},{6,2},{7,3},{8,12},{9,13},{10,... | collective-permute-start | bytes 638984 | tf_op jit(solution)/shard_map/ppermute | solution.py:106

commit v2 on v1

--- a/solution.py
+++ b/solution.py
@@ -15,7 +15,7 @@
     return pltpu.with_memory_space_constraint(x, VMEM)
 
 
-def prepare_kernel(points_ref, lengthscale_ref, target_ref, probes_ref, block_ref):
+def prepare_kernel(points_ref, lengthscale_ref, target_ref, probes_ref, noise_ref, block_ref, base_ref):
     features = points_ref.shape[0]
     wide = jnp.broadcast_to(lengthscale_ref[...], (features, features))
     row = lax.broadcasted_iota(jnp.int32, wide.shape, 0)
@@ -24,7 +24,9 @@
     scaled = points_ref[...] / scale
     signs = (2 * probes_ref[...] - 1).astype(jnp.float32)
     block = jnp.concatenate([scaled, target_ref[...], signs], axis=0)
-    block_ref[...] = block.astype(jnp.bfloat16)
+    block = block.astype(jnp.bfloat16)
+    block_ref[...] = block
+    base_ref[...] = noise_ref[...] * block[features:].astype(jnp.float32)
 
 
 def augmented(block, features, own):
@@ -42,13 +44,11 @@
     return x.astype(jnp.bfloat16)
 
 
-def add_blocks(features, counts, last, *refs):
-    piece_refs, rest = refs[: len(counts)], refs[len(counts) :]
-    own_ref, rest = rest[0], rest[1:]
-    noise_ref, rest = (rest[0], rest[1:]) if last else (None, rest)
-    sum_ref, out_ref = rest if len(rest) == 2 else (None, rest[0])
-    own = own_ref[...]
-    own_side = augmented(own, features, True)
+def add_blocks(features, counts, *refs):
+    piece_refs = refs[: len(counts)]
+    own_ref, out_ref = refs[len(counts)], refs[-1]
+    total = refs[len(counts) + 1][...] if len(refs) == len(counts) + 3 else None
+    own_side = augmented(own_ref[...], features, True)
     blocks = [(ref, k) for ref, count in zip(piece_refs, counts) for k in range(count)]
     low = features // 16 * 16
 
@@ -60,7 +60,7 @@
             preferred_element_type=jnp.float32,
         )
 
-    total = None
+    found = None
     ahead = exponent(*blocks[0])
     for at, (ref, k) in enumerate(blocks):
         now = ahead
@@ -68,33 +68,24 @@
             ahead = exponent(*blocks[at + 1])
         kernel = jnp.exp(now).astype(jnp.bfloat16)
         term = jnp.dot(ref[k][low:], kernel, preferred_element_type=jnp.float32)
-        total = term if total is None else total + term
-    total = total[features - low :]
-    if sum_ref is not None:
-        total = total + sum_ref[...]
-    if last:
-        total = total + noise_ref[...] * own[features:].astype(jnp.float32)
-    out_ref[...] = total
+        found = term if found is None else found + term
+    found = found[features - low :]
+    out_ref[...] = found if total is None else total + found
 
 
-def add(features, pieces, own, noise=None, total=None):
+def add(features, pieces, own, total=None):
     rows, width = own.shape
     counts = tuple(piece.shape[0] for piece in pieces)
-    last = noise is not None
-    operands = [near(piece) for piece in pieces] + [near(own)]
-    if last:
-        operands.append(noise)
-    if total is not None:
-        operands.append(near(total))
+    operands = [near(x) for x in (*pieces, own, total) if x is not None]
     shape = (rows - features, width)
-    out = jax.ShapeDtypeStruct(shape, jnp.float32) if last else VMEM(shape, jnp.float32)
+    out = VMEM(shape, jnp.float32)
     work = sum(counts) * width * width
     return pl.pallas_call(
-        functools.partial(add_blocks, features, counts, last),
+        functools.partial(add_blocks, features, counts),
         out_shape=out,
         in_specs=[IN_VMEM] * len(operands),
         out_specs=IN_VMEM,
-        cost_estimate=pl.CostEstimate(flops=2 * work * 512, bytes_accessed=0, transcendentals=work),
+        cost_estimate=pl.CostEstimate(flops=20 * work * 512, bytes_accessed=0, transcendentals=work),
     )(*operands)
 
 
@@ -118,20 +109,23 @@
     features, width = points.shape
     rows, cols = mesh_shape
     vectors = probes.shape[0] + 1
-    block = pl.pallas_call(
+    block, base = pl.pallas_call(
         prepare_kernel,
-        out_shape=VMEM((features + vectors, width), jnp.bfloat16),
-        in_specs=[IN_VMEM] * 4,
-        out_specs=IN_VMEM,
-    )(points, lengthscale[None, :], target[None, :], probes)
+        out_shape=(VMEM((features + vectors, width), jnp.bfloat16), VMEM((vectors, width), jnp.float32)),
+        in_specs=[IN_VMEM] * 5,
+        out_specs=(IN_VMEM, IN_VMEM),
+    )(points, lengthscale[None, :], target[None, :], probes, noise[None, :])
+    peer = swap(block, mesh_shape, 3, 0)
     mine = block[None]
     for bits in powers(cols):
         mine = jnp.concatenate([mine, swap(mine, mesh_shape, 1, bits)], axis=0)
-    for bits in powers(rows)[:-1]:
+    for bits in powers(rows)[:-2]:
         mine = jnp.concatenate([mine, swap(mine, mesh_shape, bits + 1, 0)], axis=0)
     other = swap(mine, mesh_shape, 1, 0)
-    total = add(features, [mine], block)
-    return add(features, [other], block, noise[None, :], total)
+    partial = add(features, [mine], peer)
+    partial = add(features, [other], peer, partial)
+    total = add(features, [mine, other], block, base)
+    return total + swap(partial, mesh_shape, 3, 0)
 
 
 def solution(mesh):

time: 21.4 us -> 17.3 us (0.81)
  the two profiles are of different devices: /device:TPU:25 before, /device:TPU:0 now
where the time goes in v2:
time: 17.3 us; the launch traced here: 17.2 us
  starting transfers between devices  8.94 us (52%)
  Pallas kernels  4.33 us (25%)
  waiting for transfers between devices  3.23 us (19%)
  other arithmetic  0.64 us (4%)
    ppermute x5, starting transfers between devices, swap(): return lax.ppermute(x, ('rows', 'cols'), pairs)  8.94 us
    pallas_call x3, Pallas kernels, add(): pl.pallas_call(functools.partial(add_blocks, features, counts), out_shape...  3.41 us
    ppermute x5, waiting for transfers between devices, swap(): return lax.ppermute(x, ('rows', 'cols'), pairs)  3.23 us
    pallas_call x1, Pallas kernels, local(): pl.pallas_call(prepare_kernel, out_shape=(VMEM((features + vectors, width...  0.92 us
    add x1, other arithmetic, local(): return total + swap(partial, mesh_shape, 3, 0)  0.61 us
  transfers between devices with their start and end apart: 5, of which 3 were waited for; matrix products, arithmetic and copies ran while one was open for 0% of the time, Pallas kernels for 14%

profile of v2, /device:TPU:0, one launch (start us, length us, event | category | flops | bytes accessed | tf_op | source)
XLA Modules:
  0.0 17.2 jit_solution(17618742760135968030)
XLA Ops:
  0.0 0.9 %shard_map.55 = (bf16[32,416]{1,0:T(8,128)(2,1)S(1)}, f32[8,416]{1,0:T(8,128)S(1)}) custom-call(f32[24,416]{1,0:T(8,128)} %points_ref.1, f32[1,24]{1,0:T(1,128)} %bitcast.9, f32[1,416]{1,0:T(1,128)} %bitcast.7, s32[7,416]{1,0:T(8,128)} %probes_ref.1, f32[1,416]{1,0:T(1,128)} %bitcast.8), custom_call_target="tpu_custom_call" | custom-call | tf_op jit(solution)/shard_map/pallas_call | solution.py:112
  0.9 3.5 %collective-permute-start = (bf16[1,32,416]{2,1,0:T(8,128)(2,1)S(1)}, bf16[1,32,416]{2,1,0:T(8,128)(2,1)S(1)}, u32[]{:S(2)}, u32[]{:S(2)}) collective-permute-start(bf16[1,32,416]{2,1,0:T(8,128)(2,1)S(1)} %bitcast.4), channel_id=1, source_target_pairs={{0,6},{1,7},{2,4},{3,5},{4,2},{5,3},{6,0},{7,1},{8,14},{9,15},{10,... | collective-permute-start | bytes 79880 | tf_op jit(solution)/shard_map/ppermute | solution.py:97
  4.5 1.8 %collective-permute-done = bf16[1,32,416]{2,1,0:T(8,128)(2,1)S(1)} collective-permute-done((bf16[1,32,416]{2,1,0:T(8,128)(2,1)S(1)}, bf16[1,32,416]{2,1,0:T(8,128)(2,1)S(1)}, u32[]{:S(2)}, u32[]{:S(2)}) %collective-permute-start) | collective-permute-done | bytes 26656 | tf_op jit(solution)/shard_map/ppermute | solution.py:97
  6.3 1.9 %collective-permute-start.1 = (bf16[2,32,416]{2,1,0:T(8,128)(2,1)S(1)}, bf16[2,32,416]{2,1,0:T(8,128)(2,1)S(1)}, u32[]{:S(2)}, u32[]{:S(2)}) collective-permute-start(bf16[2,32,416]{2,1,0:T(8,128)(2,1)S(1)} %pad_maximum_fusion.1), channel_id=1, source_target_pairs={{0,5},{1,4},{2,7},{3,6},{4,1},{5,0},{6,3},{7,2},{8,13},{9,12},{10,... | collective-permute-start | bytes 159752 | tf_op jit(solution)/shard_map/ppermute | solution.py:97
  8.2 1.6 %collective-permute-start.3 = (bf16[32,416]{1,0:T(8,128)(2,1)S(1)}, bf16[32,416]{1,0:T(8,128)(2,1)S(1)}, u32[]{:S(2)}, u32[]{:S(2)}) collective-permute-start(bf16[32,416]{1,0:T(8,128)(2,1)S(1)} %get-tuple-element.7.refs_2_), channel_id=1, source_target_pairs={{0,12},{1,13},{2,14},{3,15},{4,8},{5,9},{6,10},{7,11},{8,4},{9,5},... | collective-permute-start | bytes 79880 | tf_op jit(solution)/shard_map/ppermute | solution.py:97
  9.7 0.6 %collective-permute-done.1 = bf16[2,32,416]{2,1,0:T(8,128)(2,1)S(1)} collective-permute-done((bf16[2,32,416]{2,1,0:T(8,128)(2,1)S(1)}, bf16[2,32,416]{2,1,0:T(8,128)(2,1)S(1)}, u32[]{:S(2)}, u32[]{:S(2)}) %collective-permute-start.1) | collective-permute-done | bytes 53280 | tf_op jit(solution)/shard_map/ppermute | solution.py:97
  10.4 0.3 %collective-permute-start.2 = (bf16[4,32,416]{2,1,0:T(8,128)(2,1)S(1)}, bf16[4,32,416]{2,1,0:T(8,128)(2,1)S(1)}, u32[]{:S(2)}, u32[]{:S(2)}) collective-permute-start(bf16[4,32,416]{2,1,0:T(8,128)(2,1)S(1)} %pad_maximum_fusion.refs_0_), channel_id=1, source_target_pairs={{0,4},{1,5},{2,6},{3,7},{4,0},{5,1},{6,2},{7,3},{8,12},{9,13},{10,... | collective-permute-start | bytes 319496 | tf_op jit(solution)/shard_map/ppermute | solution.py:97
  10.7 0.8 %collective-permute-done.3.refs_1_ = bf16[32,416]{1,0:T(8,128)(2,1)S(1)} collective-permute-done((bf16[32,416]{1,0:T(8,128)(2,1)S(1)}, bf16[32,416]{1,0:T(8,128)(2,1)S(1)}, u32[]{:S(2)}, u32[]{:S(2)}) %collective-permute-start.3) | collective-permute-done | bytes 26656 | tf_op jit(solution)/shard_map/ppermute | solution.py:97
  11.5 0.8 %shard_map.57.refs_2_ = f32[8,416]{1,0:T(8,128)S(1)} custom-call(bf16[4,32,416]{2,1,0:T(8,128)(2,1)S(1)} %pad_maximum_fusion.refs_0_, bf16[32,416]{1,0:T(8,128)(2,1)S(1)} %collective-permute-done.3.refs_1_), custom_call_target="tpu_custom_call" | custom-call | flops 7088373760 | tf_op jit(solution)/shard_map/pallas_call | solution.py:83
  12.3 0.0 collective-permute-done.2.refs_1_.refs_0_
  12.3 1.0 %shard_map.58 = f32[8,416]{1,0:T(8,128)S(1)} custom-call(bf16[4,32,416]{2,1,0:T(8,128)(2,1)S(1)} %collective-permute-done.2.refs_1_.refs_0_, bf16[32,416]{1,0:T(8,128)(2,1)S(1)} %collective-permute-done.3.refs_1_, f32[8,416]{1,0:T(8,128)S(1)} %shard_map.57.refs_2_), custom_call_target="tpu_custom_call" | custom-call | flops 7088373760 | tf_op jit(solution)/shard_map/pallas_call | solution.py:83
  13.3 1.6 %collective-permute-start.4 = (f32[8,416]{1,0:T(8,128)S(1)}, f32[8,416]{1,0:T(8,128)S(1)}, u32[]{:S(2)}, u32[]{:S(2)}) collective-permute-start(f32[8,416]{1,0:T(8,128)S(1)} %shard_map.58), channel_id=1, source_target_pairs={{0,12},{1,13},{2,14},{3,15},{4,8},{5,9},{6,10},{7,11},{8,4},{9,5},... | collective-permute-start | bytes 39944 | tf_op jit(solution)/shard_map/ppermute | solution.py:97
  14.9 1.6 %shard_map.56 = f32[8,416]{1,0:T(8,128)S(1)} custom-call(bf16[4,32,416]{2,1,0:T(8,128)(2,1)S(1)} %pad_maximum_fusion.refs_0_, bf16[4,32,416]{2,1,0:T(8,128)(2,1)S(1)} %collective-permute-done.2.refs_1_.refs_0_, bf16[32,416]{1,0:T(8,128)(2,1)S(1)} %get-tuple-element.7.refs_2_, f32[8,416]{1,0:T(8,128)S(1)} %get-tuple-element.8.refs_3_), custom_call_target="tpu_custom_call" | custom-call | flops 14176747520 | tf_op jit(solution)/shard_map/pallas_call | solution.py:83
  16.5 0.0 collective-permute-done.4
  16.6 0.6 %add.3 = f32[8,416]{1,0:T(8,128)} add(f32[8,416]{1,0:T(8,128)S(1)} %shard_map.56, f32[8,416]{1,0:T(8,128)S(1)} %collective-permute-done.4) | non-fusion elementwise | flops 3328 | bytes 39936 | tf_op jit(solution)/shard_map/add | solution.py:128
  (2 shorter events, 0.0 us)
Async XLA Ops:
  0.9 5.3 %collective-permute-start = (bf16[1,32,416]{2,1,0:T(8,128)(2,1)S(1)}, bf16[1,32,416]{2,1,0:T(8,128)(2,1)S(1)}, u32[]{:S(2)}, u32[]{:S(2)}) collective-permute-start(bf16[1,32,416]{2,1,0:T(8,128)(2,1)S(1)} %bitcast.4), channel_id=1, source_target_pairs={{0,6},{1,7},{2,4},{3,5},{4,2},{5,3},{6,0},{7,1},{8,14},{9,15},{10,... | collective-permute-start | bytes 79880 | tf_op jit(solution)/shard_map/ppermute | solution.py:97
  6.3 4.1 %collective-permute-start.1 = (bf16[2,32,416]{2,1,0:T(8,128)(2,1)S(1)}, bf16[2,32,416]{2,1,0:T(8,128)(2,1)S(1)}, u32[]{:S(2)}, u32[]{:S(2)}) collective-permute-start(bf16[2,32,416]{2,1,0:T(8,128)(2,1)S(1)} %pad_maximum_fusion.1), channel_id=1, source_target_pairs={{0,5},{1,4},{2,7},{3,6},{4,1},{5,0},{6,3},{7,2},{8,13},{9,12},{10,... | collective-permute-start | bytes 159752 | tf_op jit(solution)/shard_map/ppermute | solution.py:97
  8.2 3.3 %collective-permute-start.3 = (bf16[32,416]{1,0:T(8,128)(2,1)S(1)}, bf16[32,416]{1,0:T(8,128)(2,1)S(1)}, u32[]{:S(2)}, u32[]{:S(2)}) collective-permute-start(bf16[32,416]{1,0:T(8,128)(2,1)S(1)} %get-tuple-element.7.refs_2_), channel_id=1, source_target_pairs={{0,12},{1,13},{2,14},{3,15},{4,8},{5,9},{6,10},{7,11},{8,4},{9,5},... | collective-permute-start | bytes 79880 | tf_op jit(solution)/shard_map/ppermute | solution.py:97
  10.4 1.9 %collective-permute-start.2 = (bf16[4,32,416]{2,1,0:T(8,128)(2,1)S(1)}, bf16[4,32,416]{2,1,0:T(8,128)(2,1)S(1)}, u32[]{:S(2)}, u32[]{:S(2)}) collective-permute-start(bf16[4,32,416]{2,1,0:T(8,128)(2,1)S(1)} %pad_maximum_fusion.refs_0_), channel_id=1, source_target_pairs={{0,4},{1,5},{2,6},{3,7},{4,0},{5,1},{6,2},{7,3},{8,12},{9,13},{10,... | collective-permute-start | bytes 319496 | tf_op jit(solution)/shard_map/ppermute | solution.py:97
  13.3 3.2 %collective-permute-start.4 = (f32[8,416]{1,0:T(8,128)S(1)}, f32[8,416]{1,0:T(8,128)S(1)}, u32[]{:S(2)}, u32[]{:S(2)}) collective-permute-start(f32[8,416]{1,0:T(8,128)S(1)} %shard_map.58), channel_id=1, source_target_pairs={{0,12},{1,13},{2,14},{3,15},{4,8},{5,9},{6,10},{7,11},{8,4},{9,5},... | collective-permute-start | bytes 39944 | tf_op jit(solution)/shard_map/ppermute | solution.py:97

commit v3 on v2

--- a/solution.py
+++ b/solution.py
@@ -9,6 +9,8 @@
 
 VMEM = pltpu.VMEM
 IN_VMEM = pl.BlockSpec(memory_space=VMEM)
+CHUNK = 256
+AHEAD = 2
 
 
 def near(x):
@@ -49,25 +51,29 @@
     own_ref, out_ref = refs[len(counts)], refs[-1]
     total = refs[len(counts) + 1][...] if len(refs) == len(counts) + 3 else None
     own_side = augmented(own_ref[...], features, True)
+    width = own_ref.shape[1]
+    low = features // 16 * 16
     blocks = [(ref, k) for ref, count in zip(piece_refs, counts) for k in range(count)]
-    low = features // 16 * 16
+    chunks = [(at, lo, min(lo + CHUNK, width)) for at in range(len(blocks)) for lo in range(0, width, CHUNK)]
+    sides = {}
 
-    def exponent(ref, k):
+    def exponent(at, lo, hi):
+        if at not in sides:
+            ref, k = blocks[at]
+            sides[at] = augmented(ref[k], features, False)
         return lax.dot_general(
-            augmented(ref[k], features, False),
-            own_side,
-            (((0,), (0,)), ((), ())),
-            preferred_element_type=jnp.float32,
+            sides[at][:, lo:hi], own_side, (((0,), (0,)), ((), ())), preferred_element_type=jnp.float32
         )
 
     found = None
-    ahead = exponent(*blocks[0])
-    for at, (ref, k) in enumerate(blocks):
-        now = ahead
-        if at + 1 < len(blocks):
-            ahead = exponent(*blocks[at + 1])
+    ahead = [exponent(*chunk) for chunk in chunks[:AHEAD]]
+    for step, (at, lo, hi) in enumerate(chunks):
+        now = ahead.pop(0)
+        if step + AHEAD < len(chunks):
+            ahead.append(exponent(*chunks[step + AHEAD]))
         kernel = jnp.exp(now).astype(jnp.bfloat16)
-        term = jnp.dot(ref[k][low:], kernel, preferred_element_type=jnp.float32)
+        ref, k = blocks[at]
+        term = jnp.dot(ref[k][low:, lo:hi], kernel, preferred_element_type=jnp.float32)
         found = term if found is None else found + term
     found = found[features - low :]
     out_ref[...] = found if total is None else total + found
@@ -115,16 +121,19 @@
         in_specs=[IN_VMEM] * 5,
         out_specs=(IN_VMEM, IN_VMEM),
     )(points, lengthscale[None, :], target[None, :], probes, noise[None, :])
+    steps = [(1, bits) for bits in powers(cols)] + [(bits + 1, 0) for bits in powers(rows)[:-2]]
     peer = swap(block, mesh_shape, 3, 0)
-    mine = block[None]
-    for bits in powers(cols):
-        mine = jnp.concatenate([mine, swap(mine, mesh_shape, 1, bits)], axis=0)
-    for bits in powers(rows)[:-2]:
-        mine = jnp.concatenate([mine, swap(mine, mesh_shape, bits + 1, 0)], axis=0)
-    other = swap(mine, mesh_shape, 1, 0)
-    partial = add(features, [mine], peer)
-    partial = add(features, [other], peer, partial)
-    total = add(features, [mine, other], block, base)
+    early = block[None]
+    for step in steps[:-1]:
+        early = jnp.concatenate([early, swap(early, mesh_shape, *step)], axis=0)
+    late = swap(early, mesh_shape, *steps[-1])
+    partial = add(features, [early], peer)
+    sent, partial = lax.optimization_barrier((early, partial))
+    early_other = swap(sent, mesh_shape, 1, 0)
+    late_other = swap(late, mesh_shape, 1, 0)
+    partial = add(features, [early_other, late], peer, partial)
+    partial = add(features, [late_other], peer, partial)
+    total = add(features, [early, early_other, late, late_other], block, base)
     return total + swap(partial, mesh_shape, 3, 0)
 
 

time: 17.3 us -> 16.4 us (0.948)
  waiting for transfers between devices: 3.23 us -> 1.58 us
  starting transfers between devices: 8.94 us -> 9.97 us
  Pallas kernels: 4.33 us -> 3.9 us
    ppermute x5 -> x6, waiting for transfers between devices: 3.23 us -> 1.58 us  [swap(): return lax.ppermute(x, ('rows', 'cols'), pairs)]
    ppermute x5 -> x6, starting transfers between devices: 8.94 us -> 9.97 us  [swap(): return lax.ppermute(x, ('rows', 'cols'), pairs)]
    pallas_call x3 -> x4, Pallas kernels: 3.41 us -> 2.98 us  [add(): pl.pallas_call(functools.partial(add_blocks, features, counts), out_shape...]
  transfers between devices with their start and end apart: 5 -> 6, of which waited for: 3 -> 3; matrix products, arithmetic and copies ran while one was open for 0% -> 0% of each run, Pallas kernels for 14% -> 16%
where the time goes in v3:
time: 16.4 us; the launch traced here: 16.1 us
  starting transfers between devices  9.97 us (61%)
  Pallas kernels  3.9 us (24%)
  waiting for transfers between devices  1.58 us (10%)
  other arithmetic  0.62 us (4%)
    ppermute x6, starting transfers between devices, swap(): return lax.ppermute(x, ('rows', 'cols'), pairs)  9.97 us
    pallas_call x4, Pallas kernels, add(): pl.pallas_call(functools.partial(add_blocks, features, counts), out_shape...  2.98 us
    ppermute x6, waiting for transfers between devices, swap(): return lax.ppermute(x, ('rows', 'cols'), pairs)  1.58 us
    pallas_call x1, Pallas kernels, local(): pl.pallas_call(prepare_kernel, out_shape=(VMEM((features + vectors, width...  0.92 us
    add x1, other arithmetic, local(): return total + swap(partial, mesh_shape, 3, 0)  0.61 us
  transfers between devices with their start and end apart: 6, of which 3 were waited for; matrix products, arithmetic and copies ran while one was open for 0% of the time, Pallas kernels for 16%

profile of v3, /device:TPU:0, one launch (start us, length us, event | category | flops | bytes accessed | tf_op | source)
XLA Modules:
  0.0 16.1 jit_solution(6315273901064216623)
XLA Ops:
  0.0 0.9 %shard_map.55 = (bf16[32,416]{1,0:T(8,128)(2,1)S(1)}, f32[8,416]{1,0:T(8,128)S(1)}) custom-call(f32[24,416]{1,0:T(8,128)} %points_ref.1, f32[1,24]{1,0:T(1,128)} %bitcast.8, f32[1,416]{1,0:T(1,128)} %bitcast.6, s32[7,416]{1,0:T(8,128)} %probes_ref.1, f32[1,416]{1,0:T(1,128)} %bitcast.7), custom_call_target="tpu_custom_call" | custom-call | tf_op jit(solution)/shard_map/pallas_call | solution.py:118
  0.9 3.5 %collective-permute-start = (bf16[1,32,416]{2,1,0:T(8,128)(2,1)S(1)}, bf16[1,32,416]{2,1,0:T(8,128)(2,1)S(1)}, u32[]{:S(2)}, u32[]{:S(2)}) collective-permute-start(bf16[1,32,416]{2,1,0:T(8,128)(2,1)S(1)} %bitcast.4), channel_id=1, source_target_pairs={{0,6},{1,7},{2,4},{3,5},{4,2},{5,3},{6,0},{7,1},{8,14},{9,15},{10,... | collective-permute-start | bytes 79880 | tf_op jit(solution)/shard_map/ppermute | solution.py:103
  4.5 1.8 %collective-permute-start.1 = (bf16[32,416]{1,0:T(8,128)(2,1)S(1)}, bf16[32,416]{1,0:T(8,128)(2,1)S(1)}, u32[]{:S(2)}, u32[]{:S(2)}) collective-permute-start(bf16[32,416]{1,0:T(8,128)(2,1)S(1)} %get-tuple-element.9.refs_4_), channel_id=1, source_target_pairs={{0,12},{1,13},{2,14},{3,15},{4,8},{5,9},{6,10},{7,11},{8,4},{9,5},... | collective-permute-start | bytes 79880 | tf_op jit(solution)/shard_map/ppermute | solution.py:103
  6.3 0.0 collective-permute-done
  6.3 1.9 %collective-permute-start.3 = (bf16[2,32,416]{2,1,0:T(8,128)(2,1)S(1)}, bf16[2,32,416]{2,1,0:T(8,128)(2,1)S(1)}, u32[]{:S(2)}, u32[]{:S(2)}) collective-permute-start(bf16[2,32,416]{2,1,0:T(8,128)(2,1)S(1)} %pad_maximum_fusion.refs_0_), channel_id=1, source_target_pairs={{0,5},{1,4},{2,7},{3,6},{4,1},{5,0},{6,3},{7,2},{8,13},{9,12},{10,... | collective-permute-start | bytes 159752 | tf_op jit(solution)/shard_map/ppermute | solution.py:103
  8.2 0.0 collective-permute-done.1.refs_1_.refs_2_
  8.2 0.4 %shard_map.56.refs_3_ = f32[8,416]{1,0:T(8,128)S(1)} custom-call(bf16[2,32,416]{2,1,0:T(8,128)(2,1)S(1)} %pad_maximum_fusion.refs_0_, bf16[32,416]{1,0:T(8,128)(2,1)S(1)} %collective-permute-done.1.refs_1_.refs_2_), custom_call_target="tpu_custom_call" | custom-call | flops 3544186880 | tf_op jit(solution)/shard_map/pallas_call | solution.py:89
  8.6 0.5 %collective-permute-start.2 = (bf16[2,32,416]{2,1,0:T(8,128)(2,1)S(1)}, bf16[2,32,416]{2,1,0:T(8,128)(2,1)S(1)}, u32[]{:S(2)}, u32[]{:S(2)}) collective-permute-start(bf16[2,32,416]{2,1,0:T(8,128)(2,1)S(1)} %pad_maximum_fusion.refs_0_), channel_id=1, source_target_pairs={{0,4},{1,5},{2,6},{3,7},{4,0},{5,1},{6,2},{7,3},{8,12},{9,13},{10,... | collective-permute-start | bytes 159752 | tf_op jit(solution)/shard_map/ppermute | solution.py:103
  9.1 1.2 %collective-permute-done.3.refs_2_.refs_1_ = bf16[2,32,416]{2,1,0:T(8,128)(2,1)S(1)} collective-permute-done((bf16[2,32,416]{2,1,0:T(8,128)(2,1)S(1)}, bf16[2,32,416]{2,1,0:T(8,128)(2,1)S(1)}, u32[]{:S(2)}, u32[]{:S(2)}) %collective-permute-start.3) | collective-permute-done | bytes 53280 | tf_op jit(solution)/shard_map/ppermute | solution.py:103
  10.4 0.3 %collective-permute-start.4 = (bf16[2,32,416]{2,1,0:T(8,128)(2,1)S(1)}, bf16[2,32,416]{2,1,0:T(8,128)(2,1)S(1)}, u32[]{:S(2)}, u32[]{:S(2)}) collective-permute-start(bf16[2,32,416]{2,1,0:T(8,128)(2,1)S(1)} %collective-permute-done.3.refs_2_.refs_1_), channel_id=1, source_target_pairs={{0,4},{1,5},{2,6},{3,7},{4,0},{5,1},{6,2},{7,3},{8,12},{9,13},{10,... | collective-permute-start | bytes 159752 | tf_op jit(solution)/shard_map/ppermute | solution.py:103
  10.6 0.0 collective-permute-done.2.refs_1_.refs_0_
  10.6 0.8 %shard_map.58.refs_2_ = f32[8,416]{1,0:T(8,128)S(1)} custom-call(bf16[2,32,416]{2,1,0:T(8,128)(2,1)S(1)} %collective-permute-done.2.refs_1_.refs_0_, bf16[2,32,416]{2,1,0:T(8,128)(2,1)S(1)} %collective-permute-done.3.refs_2_.refs_1_, bf16[32,416]{1,0:T(8,128)(2,1)S(1)} %collective-permute-done.1.refs_1_.refs_2_, f32[8,416]{1,0:T(8,128)S(1)} %shard_map.56.refs_3_), custom_call_target="tpu_custom_call" | custom-call | flops 7088373760 | tf_op jit(solution)/shard_map/pallas_call | solution.py:89
  11.4 0.2 %collective-permute-done.4.refs_3_.refs_0_ = bf16[2,32,416]{2,1,0:T(8,128)(2,1)S(1)} collective-permute-done((bf16[2,32,416]{2,1,0:T(8,128)(2,1)S(1)}, bf16[2,32,416]{2,1,0:T(8,128)(2,1)S(1)}, u32[]{:S(2)}, u32[]{:S(2)}) %collective-permute-start.4) | collective-permute-done | bytes 53280 | tf_op jit(solution)/shard_map/ppermute | solution.py:103
  11.6 0.5 %shard_map.59 = f32[8,416]{1,0:T(8,128)S(1)} custom-call(bf16[2,32,416]{2,1,0:T(8,128)(2,1)S(1)} %collective-permute-done.4.refs_3_.refs_0_, bf16[32,416]{1,0:T(8,128)(2,1)S(1)} %collective-permute-done.1.refs_1_.refs_2_, f32[8,416]{1,0:T(8,128)S(1)} %shard_map.58.refs_2_), custom_call_target="tpu_custom_call" | custom-call | flops 3544186880 | tf_op jit(solution)/shard_map/pallas_call | solution.py:89
  12.1 2.0 %collective-permute-start.5 = (f32[8,416]{1,0:T(8,128)S(1)}, f32[8,416]{1,0:T(8,128)S(1)}, u32[]{:S(2)}, u32[]{:S(2)}) collective-permute-start(f32[8,416]{1,0:T(8,128)S(1)} %shard_map.59), channel_id=1, source_target_pairs={{0,12},{1,13},{2,14},{3,15},{4,8},{5,9},{6,10},{7,11},{8,4},{9,5},... | collective-permute-start | bytes 39944 | tf_op jit(solution)/shard_map/ppermute | solution.py:103
  14.1 1.3 %shard_map.57 = f32[8,416]{1,0:T(8,128)S(1)} custom-call(bf16[2,32,416]{2,1,0:T(8,128)(2,1)S(1)} %pad_maximum_fusion.refs_0_, bf16[2,32,416]{2,1,0:T(8,128)(2,1)S(1)} %collective-permute-done.2.refs_1_.refs_0_, bf16[2,32,416]{2,1,0:T(8,128)(2,1)S(1)} %collective-permute-done.3.refs_2_.refs_1_, ...), custom_call_target="tpu_custom_call" | custom-call | flops 14176747520 | tf_op jit(solution)/shard_map/pallas_call | solution.py:89
  15.3 0.2 collective-permute-done.5
  15.5 0.6 %add.3 = f32[8,416]{1,0:T(8,128)} add(f32[8,416]{1,0:T(8,128)S(1)} %shard_map.57, f32[8,416]{1,0:T(8,128)S(1)} %collective-permute-done.5) | non-fusion elementwise | flops 3328 | bytes 39936 | tf_op jit(solution)/shard_map/add | solution.py:137
  (1 shorter events, 0.0 us)
Async XLA Ops:
  0.9 5.3 %collective-permute-start = (bf16[1,32,416]{2,1,0:T(8,128)(2,1)S(1)}, bf16[1,32,416]{2,1,0:T(8,128)(2,1)S(1)}, u32[]{:S(2)}, u32[]{:S(2)}) collective-permute-start(bf16[1,32,416]{2,1,0:T(8,128)(2,1)S(1)} %bitcast.4), channel_id=1, source_target_pairs={{0,6},{1,7},{2,4},{3,5},{4,2},{5,3},{6,0},{7,1},{8,14},{9,15},{10,... | collective-permute-start | bytes 79880 | tf_op jit(solution)/shard_map/ppermute | solution.py:103
  4.5 3.7 %collective-permute-start.1 = (bf16[32,416]{1,0:T(8,128)(2,1)S(1)}, bf16[32,416]{1,0:T(8,128)(2,1)S(1)}, u32[]{:S(2)}, u32[]{:S(2)}) collective-permute-start(bf16[32,416]{1,0:T(8,128)(2,1)S(1)} %get-tuple-element.9.refs_4_), channel_id=1, source_target_pairs={{0,12},{1,13},{2,14},{3,15},{4,8},{5,9},{6,10},{7,11},{8,4},{9,5},... | collective-permute-start | bytes 79880 | tf_op jit(solution)/shard_map/ppermute | solution.py:103
  6.3 4.1 %collective-permute-start.3 = (bf16[2,32,416]{2,1,0:T(8,128)(2,1)S(1)}, bf16[2,32,416]{2,1,0:T(8,128)(2,1)S(1)}, u32[]{:S(2)}, u32[]{:S(2)}) collective-permute-start(bf16[2,32,416]{2,1,0:T(8,128)(2,1)S(1)} %pad_maximum_fusion.refs_0_), channel_id=1, source_target_pairs={{0,5},{1,4},{2,7},{3,6},{4,1},{5,0},{6,3},{7,2},{8,13},{9,12},{10,... | collective-permute-start | bytes 159752 | tf_op jit(solution)/shard_map/ppermute | solution.py:103
  8.6 2.0 %collective-permute-start.2 = (bf16[2,32,416]{2,1,0:T(8,128)(2,1)S(1)}, bf16[2,32,416]{2,1,0:T(8,128)(2,1)S(1)}, u32[]{:S(2)}, u32[]{:S(2)}) collective-permute-start(bf16[2,32,416]{2,1,0:T(8,128)(2,1)S(1)} %pad_maximum_fusion.refs_0_), channel_id=1, source_target_pairs={{0,4},{1,5},{2,6},{3,7},{4,0},{5,1},{6,2},{7,3},{8,12},{9,13},{10,... | collective-permute-start | bytes 159752 | tf_op jit(solution)/shard_map/ppermute | solution.py:103
  10.4 1.3 %collective-permute-start.4 = (bf16[2,32,416]{2,1,0:T(8,128)(2,1)S(1)}, bf16[2,32,416]{2,1,0:T(8,128)(2,1)S(1)}, u32[]{:S(2)}, u32[]{:S(2)}) collective-permute-start(bf16[2,32,416]{2,1,0:T(8,128)(2,1)S(1)} %collective-permute-done.3.refs_2_.refs_1_), channel_id=1, source_target_pairs={{0,4},{1,5},{2,6},{3,7},{4,0},{5,1},{6,2},{7,3},{8,12},{9,13},{10,... | collective-permute-start | bytes 159752 | tf_op jit(solution)/shard_map/ppermute | solution.py:103
  12.1 3.4 %collective-permute-start.5 = (f32[8,416]{1,0:T(8,128)S(1)}, f32[8,416]{1,0:T(8,128)S(1)}, u32[]{:S(2)}, u32[]{:S(2)}) collective-permute-start(f32[8,416]{1,0:T(8,128)S(1)} %shard_map.59), channel_id=1, source_target_pairs={{0,12},{1,13},{2,14},{3,15},{4,8},{5,9},{6,10},{7,11},{8,4},{9,5},... | collective-permute-start | bytes 39944 | tf_op jit(solution)/shard_map/ppermute | solution.py:103

commit v4 on v3

--- a/solution.py
+++ b/solution.py
@@ -9,7 +9,8 @@
 
 VMEM = pltpu.VMEM
 IN_VMEM = pl.BlockSpec(memory_space=VMEM)
-CHUNK = 256
+LANES = 128
+CHUNK = 2
 AHEAD = 2
 
 
@@ -17,7 +18,7 @@
     return pltpu.with_memory_space_constraint(x, VMEM)
 
 
-def prepare_kernel(points_ref, lengthscale_ref, target_ref, probes_ref, noise_ref, block_ref, base_ref):
+def prepare_kernel(points_ref, lengthscale_ref, target_ref, probes_ref, noise_ref, block_ref, base_ref, packed_ref):
     features = points_ref.shape[0]
     wide = jnp.broadcast_to(lengthscale_ref[...], (features, features))
     row = lax.broadcasted_iota(jnp.int32, wide.shape, 0)
@@ -26,6 +27,12 @@
     scaled = points_ref[...] / scale
     signs = (2 * probes_ref[...] - 1).astype(jnp.float32)
     block = jnp.concatenate([scaled, target_ref[...], signs], axis=0)
+    rows, width = block.shape
+    full = width // LANES * LANES
+    for tile in range(full // LANES):
+        packed_ref[rows * tile : rows * (tile + 1), :] = block[:, LANES * tile : LANES * (tile + 1)].astype(jnp.bfloat16)
+    high, low = block[: rows // 2, full:], block[rows // 2 :, full:]
+    packed_ref[full // LANES * rows :, :] = jnp.concatenate([high, low, high, low], axis=1).astype(jnp.bfloat16)
     block = block.astype(jnp.bfloat16)
     block_ref[...] = block
     base_ref[...] = noise_ref[...] * block[features:].astype(jnp.float32)
@@ -46,37 +53,60 @@
     return x.astype(jnp.bfloat16)
 
 
-def add_blocks(features, counts, *refs):
+def rest_tile(first, second, features):
+    rows = first.shape[0]
+    first = first.astype(jnp.float32)
+    lane = lax.broadcasted_iota(jnp.int32, (rows, LANES), 1)
+    left = lane % (LANES // 2) < LANES // 4
+    high, low = first, pltpu.roll(first, LANES - LANES // 4, 1)
+    if second is None:
+        row = lax.broadcasted_iota(jnp.int32, (rows, LANES), 0)
+        low = jnp.where(left | (row + rows < features), low, 0.0)
+    else:
+        second = second.astype(jnp.float32)
+        high = jnp.where(left, high, pltpu.roll(second, LANES // 4, 1))
+        low = jnp.where(left, low, second)
+    return jnp.concatenate([high, low], axis=0).astype(jnp.bfloat16)
+
+
+def add_pieces(features, counts, *refs):
     piece_refs = refs[: len(counts)]
     own_ref, out_ref = refs[len(counts)], refs[-1]
     total = refs[len(counts) + 1][...] if len(refs) == len(counts) + 3 else None
     own_side = augmented(own_ref[...], features, True)
-    width = own_ref.shape[1]
+    rows = own_ref.shape[0]
     low = features // 16 * 16
-    blocks = [(ref, k) for ref, count in zip(piece_refs, counts) for k in range(count)]
-    chunks = [(at, lo, min(lo + CHUNK, width)) for at in range(len(blocks)) for lo in range(0, width, CHUNK)]
-    sides = {}
+    pieces = [(ref, k) for ref, count in zip(piece_refs, counts) for k in range(count)]
+    whole = piece_refs[0].shape[1] // rows * rows
+    tiles = [(ref, k, lo) for ref, k in pieces for lo in range(0, whole, rows)]
+    tiles += [(pieces[at : at + 2],) for at in range(0, len(pieces), 2)]
+    chunks = [tiles[at : at + CHUNK] for at in range(0, len(tiles), CHUNK)]
 
-    def exponent(at, lo, hi):
-        if at not in sides:
-            ref, k = blocks[at]
-            sides[at] = augmented(ref[k], features, False)
-        return lax.dot_general(
-            sides[at][:, lo:hi], own_side, (((0,), (0,)), ((), ())), preferred_element_type=jnp.float32
+    def load(tile):
+        if len(tile) == 3:
+            ref, k, lo = tile
+            return ref[k, lo : lo + rows, :]
+        both = [ref[k, whole:, :] for ref, k in tile[0]]
+        return rest_tile(both[0], both[1] if len(both) == 2 else None, features)
+
+    def exponent(chunk):
+        block = jnp.concatenate([load(tile) for tile in chunk], axis=1)
+        side = augmented(block, features, False)
+        return block[low:], lax.dot_general(
+            side, own_side, (((0,), (0,)), ((), ())), preferred_element_type=jnp.float32
         )
 
-    found = None
-    ahead = [exponent(*chunk) for chunk in chunks[:AHEAD]]
-    for step, (at, lo, hi) in enumerate(chunks):
-        now = ahead.pop(0)
+    found = total
+    ahead = [exponent(chunk) for chunk in chunks[:AHEAD]]
+    for step in range(len(chunks)):
+        vectors, now = ahead.pop(0)
         if step + AHEAD < len(chunks):
-            ahead.append(exponent(*chunks[step + AHEAD]))
+            ahead.append(exponent(chunks[step + AHEAD]))
         kernel = jnp.exp(now).astype(jnp.bfloat16)
-        ref, k = blocks[at]
-        term = jnp.dot(ref[k][low:, lo:hi], kernel, preferred_element_type=jnp.float32)
+        term = jnp.dot(vectors, kernel, preferred_element_type=jnp.float32)
+        term = term[features - low :]
         found = term if found is None else found + term
-    found = found[features - low :]
-    out_ref[...] = found if total is None else total + found
+    out_ref[...] = found
 
 
 def add(features, pieces, own, total=None):
@@ -85,14 +115,21 @@
     operands = [near(x) for x in (*pieces, own, total) if x is not None]
     shape = (rows - features, width)
     out = VMEM(shape, jnp.float32)
-    work = sum(counts) * width * width
+    work = 2 * sum(counts) * width * width
     return pl.pallas_call(
-        functools.partial(add_blocks, features, counts),
+        functools.partial(add_pieces, features, counts),
         out_shape=out,
         in_specs=[IN_VMEM] * len(operands),
         out_specs=IN_VMEM,
         cost_estimate=pl.CostEstimate(flops=20 * work * 512, bytes_accessed=0, transcendentals=work),
     )(*operands)
+
+
+def paired(first, second):
+    whole = first.shape[0] // 32 * 32
+    lane = lax.broadcasted_iota(jnp.int32, first[whole:].shape, 1)
+    rest = jnp.where(lane < LANES // 2, first[whole:], second[whole:])
+    return jnp.concatenate([first[:whole], second[:whole], rest], axis=0)[None]
 
 
 def swap(x, mesh_shape, row_bits, col_bits):
@@ -115,16 +152,22 @@
     features, width = points.shape
     rows, cols = mesh_shape
     vectors = probes.shape[0] + 1
-    block, base = pl.pallas_call(
+    height = features + vectors
+    packed_rows = width // LANES * height + height // 2
+    block, base, packed = pl.pallas_call(
         prepare_kernel,
-        out_shape=(VMEM((features + vectors, width), jnp.bfloat16), VMEM((vectors, width), jnp.float32)),
+        out_shape=(
+            VMEM((height, width), jnp.bfloat16),
+            VMEM((vectors, width), jnp.float32),
+            VMEM((packed_rows, LANES), jnp.bfloat16),
+        ),
         in_specs=[IN_VMEM] * 5,
-        out_specs=(IN_VMEM, IN_VMEM),
+        out_specs=(IN_VMEM,) * 3,
     )(points, lengthscale[None, :], target[None, :], probes, noise[None, :])
     steps = [(1, bits) for bits in powers(cols)] + [(bits + 1, 0) for bits in powers(rows)[:-2]]
     peer = swap(block, mesh_shape, 3, 0)
-    early = block[None]
-    for step in steps[:-1]:
+    early = paired(packed, swap(packed, mesh_shape, *steps[0]))
+    for step in steps[1:-1]:
         early = jnp.concatenate([early, swap(early, mesh_shape, *step)], axis=0)
     late = swap(early, mesh_shape, *steps[-1])
     partial = add(features, [early], peer)

time: 16.4 us -> 16 us (0.976)
  waiting for transfers between devices: 1.58 us -> 1.41 us
    ppermute x6, waiting for transfers between devices: 1.58 us -> 1.41 us  [swap(): return lax.ppermute(x, ('rows', 'cols'), pairs)]
  transfers between devices with their start and end apart: 6 -> 6, of which waited for: 3 -> 3; matrix products, arithmetic and copies ran while one was open for 0% -> 0% of each run, Pallas kernels for 16% -> 15%
where the time goes in v4:
time: 16 us; the launch traced here: 15.8 us
  starting transfers between devices  9.9 us (62%)
  Pallas kernels  3.78 us (24%)
  waiting for transfers between devices  1.41 us (9%)
  other arithmetic  0.63 us (4%)
    ppermute x6, starting transfers between devices, swap(): return lax.ppermute(x, ('rows', 'cols'), pairs)  9.9 us
    pallas_call x4, Pallas kernels, add(): pl.pallas_call(functools.partial(add_pieces, features, counts), out_shape...  2.79 us
    ppermute x6, waiting for transfers between devices, swap(): return lax.ppermute(x, ('rows', 'cols'), pairs)  1.41 us
    pallas_call x1, Pallas kernels, local(): pl.pallas_call(prepare_kernel, out_shape=(VMEM((height, width), jnp.bfloa...  0.99 us
    add x1, other arithmetic, local(): return total + swap(partial, mesh_shape, 3, 0)  0.61 us
  transfers between devices with their start and end apart: 6, of which 3 were waited for; matrix products, arithmetic and copies ran while one was open for 0% of the time, Pallas kernels for 15%

profile of v4, /device:TPU:0, one launch (start us, length us, event | category | flops | bytes accessed | tf_op | source)
XLA Modules:
  0.0 15.8 jit_solution(2950990823630039794)
XLA Ops:
  0.0 1.0 %shard_map.55 = (bf16[32,416]{1,0:T(8,128)(2,1)S(1)}, f32[8,416]{1,0:T(8,128)S(1)}, bf16[112,128]{1,0:T(8,128)(2,1)S(1)}) custom-call(f32[24,416]{1,0:T(8,128)} %points_ref.1, f32[1,24]{1,0:T(1,128)} %bitcast.7, f32[1,416]{1,0:T(1,128)} %bitcast.5, s32[7,416]{1,0:T(8,128)} %probes_ref.1, f32[1,416]{1,0:T(1,128)} %bitcast.6), custom_call_target="tpu_custom_call" | custom-call | tf_op jit(solution)/shard_map/pallas_call | solution.py:157
  1.0 3.5 %collective-permute-start = (bf16[112,128]{1,0:T(8,128)(2,1)S(1)}, bf16[112,128]{1,0:T(8,128)(2,1)S(1)}, u32[]{:S(2)}, u32[]{:S(2)}) collective-permute-start(bf16[112,128]{1,0:T(8,128)(2,1)S(1)} %get-tuple-element.10), channel_id=1, source_target_pairs={{0,6},{1,7},{2,4},{3,5},{4,2},{5,3},{6,0},{7,1},{8,14},{9,15},{10,... | collective-permute-start | bytes 86024 | tf_op jit(solution)/shard_map/ppermute | solution.py:140
  4.5 1.8 %collective-permute-start.1 = (bf16[32,416]{1,0:T(8,128)(2,1)S(1)}, bf16[32,416]{1,0:T(8,128)(2,1)S(1)}, u32[]{:S(2)}, u32[]{:S(2)}) collective-permute-start(bf16[32,416]{1,0:T(8,128)(2,1)S(1)} %get-tuple-element.11.refs_4_), channel_id=1, source_target_pairs={{0,12},{1,13},{2,14},{3,15},{4,8},{5,9},{6,10},{7,11},{8,4},{9,5},... | collective-permute-start | bytes 79880 | tf_op jit(solution)/shard_map/ppermute | solution.py:140
  6.3 0.0 collective-permute-done
  6.3 1.8 %collective-permute-start.3 = (bf16[1,208,128]{2,1,0:T(8,128)(2,1)S(1)}, bf16[1,208,128]{2,1,0:T(8,128)(2,1)S(1)}, u32[]{:S(2)}, u32[]{:S(2)}) collective-permute-start(bf16[1,208,128]{2,1,0:T(8,128)(2,1)S(1)} %maximum_bitcast_fusion.refs_0_), channel_id=1, source_target_pairs={{0,5},{1,4},{2,7},{3,6},{4,1},{5,0},{6,3},{7,2},{8,13},{9,12},{10,... | collective-permute-start | bytes 159752 | tf_op jit(solution)/shard_map/ppermute | solution.py:140
  8.1 0.0 collective-permute-done.1.refs_1_.refs_2_
  8.1 0.5 %shard_map.56.refs_3_ = f32[8,416]{1,0:T(8,128)S(1)} custom-call(bf16[1,208,128]{2,1,0:T(8,128)(2,1)S(1)} %maximum_bitcast_fusion.refs_0_, bf16[32,416]{1,0:T(8,128)(2,1)S(1)} %collective-permute-done.1.refs_1_.refs_2_), custom_call_target="tpu_custom_call" | custom-call | flops 3544186880 | tf_op jit(solution)/shard_map/pallas_call | solution.py:119
  8.6 0.5 %collective-permute-start.2 = (bf16[1,208,128]{2,1,0:T(8,128)(2,1)S(1)}, bf16[1,208,128]{2,1,0:T(8,128)(2,1)S(1)}, u32[]{:S(2)}, u32[]{:S(2)}) collective-permute-start(bf16[1,208,128]{2,1,0:T(8,128)(2,1)S(1)} %maximum_bitcast_fusion.refs_0_), channel_id=1, source_target_pairs={{0,4},{1,5},{2,6},{3,7},{4,0},{5,1},{6,2},{7,3},{8,12},{9,13},{10,... | collective-permute-start | bytes 159752 | tf_op jit(solution)/shard_map/ppermute | solution.py:140
  9.1 1.0 %collective-permute-done.3.refs_2_.refs_1_ = bf16[1,208,128]{2,1,0:T(8,128)(2,1)S(1)} collective-permute-done((bf16[1,208,128]{2,1,0:T(8,128)(2,1)S(1)}, bf16[1,208,128]{2,1,0:T(8,128)(2,1)S(1)}, u32[]{:S(2)}, u32[]{:S(2)}) %collective-permute-start.3) | collective-permute-done | bytes 53280 | tf_op jit(solution)/shard_map/ppermute | solution.py:140
  10.0 0.4 %collective-permute-start.4 = (bf16[1,208,128]{2,1,0:T(8,128)(2,1)S(1)}, bf16[1,208,128]{2,1,0:T(8,128)(2,1)S(1)}, u32[]{:S(2)}, u32[]{:S(2)}) collective-permute-start(bf16[1,208,128]{2,1,0:T(8,128)(2,1)S(1)} %collective-permute-done.3.refs_2_.refs_1_), channel_id=1, source_target_pairs={{0,4},{1,5},{2,6},{3,7},{4,0},{5,1},{6,2},{7,3},{8,12},{9,13},{10,... | collective-permute-start | bytes 159752 | tf_op jit(solution)/shard_map/ppermute | solution.py:140
  10.4 0.0 collective-permute-done.2.refs_1_.refs_0_
  10.4 0.7 %shard_map.58.refs_2_ = f32[8,416]{1,0:T(8,128)S(1)} custom-call(bf16[1,208,128]{2,1,0:T(8,128)(2,1)S(1)} %collective-permute-done.2.refs_1_.refs_0_, bf16[1,208,128]{2,1,0:T(8,128)(2,1)S(1)} %collective-permute-done.3.refs_2_.refs_1_, bf16[32,416]{1,0:T(8,128)(2,1)S(1)} %collective-permute-done.1.refs_1_.refs_2_, f32[8,416]{1,0:T(8,128)S(1)} %shard_map.56.refs_3_), custom_call_target="tpu_custom_call" | custom-call | flops 7088373760 | tf_op jit(solution)/shard_map/pallas_call | solution.py:119
  11.1 0.2 %collective-permute-done.4.refs_3_.refs_0_ = bf16[1,208,128]{2,1,0:T(8,128)(2,1)S(1)} collective-permute-done((bf16[1,208,128]{2,1,0:T(8,128)(2,1)S(1)}, bf16[1,208,128]{2,1,0:T(8,128)(2,1)S(1)}, u32[]{:S(2)}, u32[]{:S(2)}) %collective-permute-start.4) | collective-permute-done | bytes 53280 | tf_op jit(solution)/shard_map/ppermute | solution.py:140
  11.3 0.5 %shard_map.59 = f32[8,416]{1,0:T(8,128)S(1)} custom-call(bf16[1,208,128]{2,1,0:T(8,128)(2,1)S(1)} %collective-permute-done.4.refs_3_.refs_0_, bf16[32,416]{1,0:T(8,128)(2,1)S(1)} %collective-permute-done.1.refs_1_.refs_2_, f32[8,416]{1,0:T(8,128)S(1)} %shard_map.58.refs_2_), custom_call_target="tpu_custom_call" | custom-call | flops 3544186880 | tf_op jit(solution)/shard_map/pallas_call | solution.py:119
  11.7 2.0 %collective-permute-start.5 = (f32[8,416]{1,0:T(8,128)S(1)}, f32[8,416]{1,0:T(8,128)S(1)}, u32[]{:S(2)}, u32[]{:S(2)}) collective-permute-start(f32[8,416]{1,0:T(8,128)S(1)} %shard_map.59), channel_id=1, source_target_pairs={{0,12},{1,13},{2,14},{3,15},{4,8},{5,9},{6,10},{7,11},{8,4},{9,5},... | collective-permute-start | bytes 39944 | tf_op jit(solution)/shard_map/ppermute | solution.py:140
  13.7 1.2 %shard_map.57 = f32[8,416]{1,0:T(8,128)S(1)} custom-call(bf16[1,208,128]{2,1,0:T(8,128)(2,1)S(1)} %maximum_bitcast_fusion.refs_0_, bf16[1,208,128]{2,1,0:T(8,128)(2,1)S(1)} %collective-permute-done.2.refs_1_.refs_0_, bf16[1,208,128]{2,1,0:T(8,128)(2,1)S(1)} %collective-permute-done.3.refs_2_.refs_1_, ...), custom_call_target="tpu_custom_call" | custom-call | flops 14176747520 | tf_op jit(solution)/shard_map/pallas_call | solution.py:119
  14.9 0.3 %collective-permute-done.5 = f32[8,416]{1,0:T(8,128)S(1)} collective-permute-done((f32[8,416]{1,0:T(8,128)S(1)}, f32[8,416]{1,0:T(8,128)S(1)}, u32[]{:S(2)}, u32[]{:S(2)}) %collective-permute-start.5) | collective-permute-done | bytes 13344 | tf_op jit(solution)/shard_map/ppermute | solution.py:140
  15.2 0.6 %add.3 = f32[8,416]{1,0:T(8,128)} add(f32[8,416]{1,0:T(8,128)S(1)} %shard_map.57, f32[8,416]{1,0:T(8,128)S(1)} %collective-permute-done.5) | non-fusion elementwise | flops 3328 | bytes 39936 | tf_op jit(solution)/shard_map/add | solution.py:180
  (5 shorter events, 0.0 us)
Async XLA Ops:
  1.0 5.3 %collective-permute-start = (bf16[112,128]{1,0:T(8,128)(2,1)S(1)}, bf16[112,128]{1,0:T(8,128)(2,1)S(1)}, u32[]{:S(2)}, u32[]{:S(2)}) collective-permute-start(bf16[112,128]{1,0:T(8,128)(2,1)S(1)} %get-tuple-element.10), channel_id=1, source_target_pairs={{0,6},{1,7},{2,4},{3,5},{4,2},{5,3},{6,0},{7,1},{8,14},{9,15},{10,... | collective-permute-start | bytes 86024 | tf_op jit(solution)/shard_map/ppermute | solution.py:140
  4.5 3.6 %collective-permute-start.1 = (bf16[32,416]{1,0:T(8,128)(2,1)S(1)}, bf16[32,416]{1,0:T(8,128)(2,1)S(1)}, u32[]{:S(2)}, u32[]{:S(2)}) collective-permute-start(bf16[32,416]{1,0:T(8,128)(2,1)S(1)} %get-tuple-element.11.refs_4_), channel_id=1, source_target_pairs={{0,12},{1,13},{2,14},{3,15},{4,8},{5,9},{6,10},{7,11},{8,4},{9,5},... | collective-permute-start | bytes 79880 | tf_op jit(solution)/shard_map/ppermute | solution.py:140
  6.3 3.7 %collective-permute-start.3 = (bf16[1,208,128]{2,1,0:T(8,128)(2,1)S(1)}, bf16[1,208,128]{2,1,0:T(8,128)(2,1)S(1)}, u32[]{:S(2)}, u32[]{:S(2)}) collective-permute-start(bf16[1,208,128]{2,1,0:T(8,128)(2,1)S(1)} %maximum_bitcast_fusion.refs_0_), channel_id=1, source_target_pairs={{0,5},{1,4},{2,7},{3,6},{4,1},{5,0},{6,3},{7,2},{8,13},{9,12},{10,... | collective-permute-start | bytes 159752 | tf_op jit(solution)/shard_map/ppermute | solution.py:140
  8.6 1.8 %collective-permute-start.2 = (bf16[1,208,128]{2,1,0:T(8,128)(2,1)S(1)}, bf16[1,208,128]{2,1,0:T(8,128)(2,1)S(1)}, u32[]{:S(2)}, u32[]{:S(2)}) collective-permute-start(bf16[1,208,128]{2,1,0:T(8,128)(2,1)S(1)} %maximum_bitcast_fusion.refs_0_), channel_id=1, source_target_pairs={{0,4},{1,5},{2,6},{3,7},{4,0},{5,1},{6,2},{7,3},{8,12},{9,13},{10,... | collective-permute-start | bytes 159752 | tf_op jit(solution)/shard_map/ppermute | solution.py:140
  10.0 1.3 %collective-permute-start.4 = (bf16[1,208,128]{2,1,0:T(8,128)(2,1)S(1)}, bf16[1,208,128]{2,1,0:T(8,128)(2,1)S(1)}, u32[]{:S(2)}, u32[]{:S(2)}) collective-permute-start(bf16[1,208,128]{2,1,0:T(8,128)(2,1)S(1)} %collective-permute-done.3.refs_2_.refs_1_), channel_id=1, source_target_pairs={{0,4},{1,5},{2,6},{3,7},{4,0},{5,1},{6,2},{7,3},{8,12},{9,13},{10,... | collective-permute-start | bytes 159752 | tf_op jit(solution)/shard_map/ppermute | solution.py:140
  11.7 3.4 %collective-permute-start.5 = (f32[8,416]{1,0:T(8,128)S(1)}, f32[8,416]{1,0:T(8,128)S(1)}, u32[]{:S(2)}, u32[]{:S(2)}) collective-permute-start(f32[8,416]{1,0:T(8,128)S(1)} %shard_map.59), channel_id=1, source_target_pairs={{0,12},{1,13},{2,14},{3,15},{4,8},{5,9},{6,10},{7,11},{8,4},{9,5},... | collective-permute-start | bytes 39944 | tf_op jit(solution)/shard_map/ppermute | solution.py:140

commit v5 on v4

--- a/solution.py
+++ b/solution.py
@@ -53,41 +53,44 @@
     return x.astype(jnp.bfloat16)
 
 
-def rest_tile(first, second, features):
-    rows = first.shape[0]
-    first = first.astype(jnp.float32)
-    lane = lax.broadcasted_iota(jnp.int32, (rows, LANES), 1)
-    left = lane % (LANES // 2) < LANES // 4
-    high, low = first, pltpu.roll(first, LANES - LANES // 4, 1)
-    if second is None:
-        row = lax.broadcasted_iota(jnp.int32, (rows, LANES), 0)
-        low = jnp.where(left | (row + rows < features), low, 0.0)
-    else:
-        second = second.astype(jnp.float32)
-        high = jnp.where(left, high, pltpu.roll(second, LANES // 4, 1))
-        low = jnp.where(left, low, second)
+def rest_tile(rests, features):
+    quarter = LANES // 4
+    rows = rests[0].shape[0]
+    rests = [rest.astype(jnp.float32) for rest in rests]
+    place = lax.broadcasted_iota(jnp.int32, (rows, LANES), 1) // quarter
+    halves = [
+        rests[at] if at + 1 >= len(rests) else jnp.where(place < 2, rests[at], rests[at + 1])
+        for at in range(0, len(rests), 2)
+    ]
+    high, low = halves[0], pltpu.roll(halves[0], LANES - quarter, 1)
+    if len(halves) == 2:
+        high = jnp.where(place % 2 == 0, high, pltpu.roll(halves[1], quarter, 1))
+        low = jnp.where(place % 2 == 0, low, halves[1])
+    row = rows + lax.broadcasted_iota(jnp.int32, (rows, LANES), 0)
+    for at, spot in enumerate((0, 2, 1, 3)):
+        if at >= len(rests):
+            low = jnp.where((place == spot) & (row >= features), 0.0, low)
     return jnp.concatenate([high, low], axis=0).astype(jnp.bfloat16)
 
 
-def add_pieces(features, counts, *refs):
+def add_blocks(features, counts, *refs):
     piece_refs = refs[: len(counts)]
     own_ref, out_ref = refs[len(counts)], refs[-1]
     total = refs[len(counts) + 1][...] if len(refs) == len(counts) + 3 else None
     own_side = augmented(own_ref[...], features, True)
     rows = own_ref.shape[0]
     low = features // 16 * 16
-    pieces = [(ref, k) for ref, count in zip(piece_refs, counts) for k in range(count)]
+    blocks = [(ref, k) for ref, count in zip(piece_refs, counts) for k in range(count)]
     whole = piece_refs[0].shape[1] // rows * rows
-    tiles = [(ref, k, lo) for ref, k in pieces for lo in range(0, whole, rows)]
-    tiles += [(pieces[at : at + 2],) for at in range(0, len(pieces), 2)]
+    tiles = [(ref, k, lo) for ref, k in blocks for lo in range(0, whole, rows)]
+    tiles += [(blocks[at : at + 4],) for at in range(0, len(blocks), 4)]
     chunks = [tiles[at : at + CHUNK] for at in range(0, len(tiles), CHUNK)]
 
     def load(tile):
         if len(tile) == 3:
             ref, k, lo = tile
             return ref[k, lo : lo + rows, :]
-        both = [ref[k, whole:, :] for ref, k in tile[0]]
-        return rest_tile(both[0], both[1] if len(both) == 2 else None, features)
+        return rest_tile([ref[k, whole:, :] for ref, k in tile[0]], features)
 
     def exponent(chunk):
         block = jnp.concatenate([load(tile) for tile in chunk], axis=1)
@@ -115,21 +118,14 @@
     operands = [near(x) for x in (*pieces, own, total) if x is not None]
     shape = (rows - features, width)
     out = VMEM(shape, jnp.float32)
-    work = 2 * sum(counts) * width * width
+    work = sum(counts) * width * width
     return pl.pallas_call(
-        functools.partial(add_pieces, features, counts),
+        functools.partial(add_blocks, features, counts),
         out_shape=out,
         in_specs=[IN_VMEM] * len(operands),
         out_specs=IN_VMEM,
-        cost_estimate=pl.CostEstimate(flops=20 * work * 512, bytes_accessed=0, transcendentals=work),
+        cost_estimate=pl.CostEstimate(flops=20480 * work, bytes_accessed=0, transcendentals=work),
     )(*operands)
-
-
-def paired(first, second):
-    whole = first.shape[0] // 32 * 32
-    lane = lax.broadcasted_iota(jnp.int32, first[whole:].shape, 1)
-    rest = jnp.where(lane < LANES // 2, first[whole:], second[whole:])
-    return jnp.concatenate([first[:whole], second[:whole], rest], axis=0)[None]
 
 
 def swap(x, mesh_shape, row_bits, col_bits):
@@ -164,19 +160,20 @@
         in_specs=[IN_VMEM] * 5,
         out_specs=(IN_VMEM,) * 3,
     )(points, lengthscale[None, :], target[None, :], probes, noise[None, :])
-    steps = [(1, bits) for bits in powers(cols)] + [(bits + 1, 0) for bits in powers(rows)[:-2]]
+    one = packed[None]
+    for step in [(1, bits) for bits in powers(cols)[:-2]] + [(bits + 1, 0) for bits in powers(rows)[:-2]]:
+        one = jnp.concatenate([one, swap(one, mesh_shape, *step)], axis=0)
     peer = swap(block, mesh_shape, 3, 0)
-    early = paired(packed, swap(packed, mesh_shape, *steps[0]))
-    for step in steps[1:-1]:
-        early = jnp.concatenate([early, swap(early, mesh_shape, *step)], axis=0)
-    late = swap(early, mesh_shape, *steps[-1])
-    partial = add(features, [early], peer)
-    sent, partial = lax.optimization_barrier((early, partial))
+    next_to, second, far = (swap(one, mesh_shape, 1, bits) for bits in (1, 2, 3))
+    early = jnp.concatenate([one, far], axis=0)
+    late = jnp.concatenate([next_to, second], axis=0)
+    total = add(features, [early], block, base)
+    sent, total = lax.optimization_barrier((early, total))
     early_other = swap(sent, mesh_shape, 1, 0)
     late_other = swap(late, mesh_shape, 1, 0)
-    partial = add(features, [early_other, late], peer, partial)
+    partial = add(features, [early, early_other, late], peer)
     partial = add(features, [late_other], peer, partial)
-    total = add(features, [early, early_other, late, late_other], block, base)
+    total = add(features, [early_other, late, late_other], block, total)
     return total + swap(partial, mesh_shape, 3, 0)
 
 

time: 16 us -> 16 us (level)
  starting transfers between devices: 9.9 us -> 8.99 us
  waiting for transfers between devices: 1.41 us -> 2.21 us
    ppermute x6 -> x7, starting transfers between devices: 9.9 us -> 8.99 us  [swap(): return lax.ppermute(x, ('rows', 'cols'), pairs)]
    ppermute x6 -> x7, waiting for transfers between devices: 1.41 us -> 2.21 us  [swap(): return lax.ppermute(x, ('rows', 'cols'), pairs)]
  transfers between devices with their start and end apart: 6 -> 7, of which waited for: 3 -> 3; matrix products, arithmetic and copies ran while one was open for 0% -> 0% of each run, Pallas kernels for 15% -> 15%
where the time goes in v5:
time: 16 us; the launch traced here: 15.8 us
  starting transfers between devices  8.99 us (56%)
  Pallas kernels  3.93 us (25%)
  waiting for transfers between devices  2.21 us (14%)
  other arithmetic  0.62 us (4%)
    ppermute x7, starting transfers between devices, swap(): return lax.ppermute(x, ('rows', 'cols'), pairs)  8.99 us
    pallas_call x4, Pallas kernels, add(): pl.pallas_call(functools.partial(add_blocks, features, counts), out_shape...  2.94 us
    ppermute x7, waiting for transfers between devices, swap(): return lax.ppermute(x, ('rows', 'cols'), pairs)  2.21 us
    pallas_call x1, Pallas kernels, local(): pl.pallas_call(prepare_kernel, out_shape=(VMEM((height, width), jnp.bfloa...  0.99 us
    add x1, other arithmetic, local(): return total + swap(partial, mesh_shape, 3, 0)  0.61 us
  transfers between devices with their start and end apart: 7, of which 3 were waited for; matrix products, arithmetic and copies ran while one was open for 0% of the time, Pallas kernels for 15%

profile of v5, /device:TPU:0, one launch (start us, length us, event | category | flops | bytes accessed | tf_op | source)
XLA Modules:
  0.0 15.8 jit_solution(3439905438496923892)
XLA Ops:
  0.0 1.0 %shard_map.55 = (bf16[32,416]{1,0:T(8,128)(2,1)S(1)}, f32[8,416]{1,0:T(8,128)S(1)}, bf16[112,128]{1,0:T(8,128)(2,1)S(1)}) custom-call(f32[24,416]{1,0:T(8,128)} %points_ref.1, f32[1,24]{1,0:T(1,128)} %bitcast.10, f32[1,416]{1,0:T(1,128)} %bitcast.8, s32[7,416]{1,0:T(8,128)} %probes_ref.1, f32[1,416]{1,0:T(1,128)} %bitcast.9), custom_call_target="tpu_custom_call" | custom-call | tf_op jit(solution)/shard_map/pallas_call | solution.py:153
  1.0 4.5 %collective-permute-start = (bf16[1,112,128]{2,1,0:T(8,128)(2,1)S(1)}, bf16[1,112,128]{2,1,0:T(8,128)(2,1)S(1)}, u32[]{:S(2)}, u32[]{:S(2)}) collective-permute-start(bf16[1,112,128]{2,1,0:T(8,128)(2,1)S(1)} %bitcast.4), channel_id=1, source_target_pairs={{0,7},{1,6},{2,5},{3,4},{4,3},{5,2},{6,1},{7,0},{8,15},{9,14},{10,... | collective-permute-start | bytes 86024 | tf_op jit(solution)/shard_map/ppermute | solution.py:136
  5.5 0.0 collective-permute-start.3
  5.5 0.9 %collective-permute-start.2 = (bf16[1,112,128]{2,1,0:T(8,128)(2,1)S(1)}, bf16[1,112,128]{2,1,0:T(8,128)(2,1)S(1)}, u32[]{:S(2)}, u32[]{:S(2)}) collective-permute-start(bf16[1,112,128]{2,1,0:T(8,128)(2,1)S(1)} %bitcast.6), channel_id=1, source_target_pairs={{0,5},{1,4},{2,7},{3,6},{4,1},{5,0},{6,3},{7,2},{8,13},{9,12},{10,... | collective-permute-start | bytes 86024 | tf_op jit(solution)/shard_map/ppermute | solution.py:136
  6.4 1.4 %collective-permute-start.5 = (bf16[32,416]{1,0:T(8,128)(2,1)S(1)}, bf16[32,416]{1,0:T(8,128)(2,1)S(1)}, u32[]{:S(2)}, u32[]{:S(2)}) collective-permute-start(bf16[32,416]{1,0:T(8,128)(2,1)S(1)} %get-tuple-element.11.refs_1_.refs_3_), channel_id=1, source_target_pairs={{0,12},{1,13},{2,14},{3,15},{4,8},{5,9},{6,10},{7,11},{8,4},{9,5},... | collective-permute-start | bytes 79880 | tf_op jit(solution)/shard_map/ppermute | solution.py:136
  7.8 0.0 collective-permute-done
  7.8 0.5 %shard_map.56.refs_4_ = f32[8,416]{1,0:T(8,128)S(1)} custom-call(bf16[2,112,128]{2,1,0:T(8,128)(2,1)S(1)} %pad_maximum_fusion.refs_0_, bf16[32,416]{1,0:T(8,128)(2,1)S(1)} %get-tuple-element.11.refs_1_.refs_3_, f32[8,416]{1,0:T(8,128)S(1)} %get-tuple-element.12.refs_2_), custom_call_target="tpu_custom_call" | custom-call | flops 7088373760 | tf_op jit(solution)/shard_map/pallas_call | solution.py:122
  8.3 0.4 %collective-permute-start.1 = (bf16[2,112,128]{2,1,0:T(8,128)(2,1)S(1)}, bf16[2,112,128]{2,1,0:T(8,128)(2,1)S(1)}, u32[]{:S(2)}, u32[]{:S(2)}) collective-permute-start(bf16[2,112,128]{2,1,0:T(8,128)(2,1)S(1)} %pad_maximum_fusion.refs_0_), channel_id=1, source_target_pairs={{0,4},{1,5},{2,6},{3,7},{4,0},{5,1},{6,2},{7,3},{8,12},{9,13},{10,... | collective-permute-start | bytes 172040 | tf_op jit(solution)/shard_map/ppermute | solution.py:136
  8.7 0.1 collective-permute-done.2
  8.8 1.1 %collective-permute-done.3 = bf16[1,112,128]{2,1,0:T(8,128)(2,1)S(1)} collective-permute-done((bf16[1,112,128]{2,1,0:T(8,128)(2,1)S(1)}, bf16[1,112,128]{2,1,0:T(8,128)(2,1)S(1)}, u32[]{:S(2)}, u32[]{:S(2)}) %collective-permute-start.3) | collective-permute-done | bytes 28704 | tf_op jit(solution)/shard_map/ppermute | solution.py:136
  10.0 0.4 %collective-permute-start.4 = (bf16[2,112,128]{2,1,0:T(8,128)(2,1)S(1)}, bf16[2,112,128]{2,1,0:T(8,128)(2,1)S(1)}, u32[]{:S(2)}, u32[]{:S(2)}) collective-permute-start(bf16[2,112,128]{2,1,0:T(8,128)(2,1)S(1)} %constant_dynamic-update-slice_fusion.refs_1_.refs_2_), channel_id=1, source_target_pairs={{0,4},{1,5},{2,6},{3,7},{4,0},{5,1},{6,2},{7,3},{8,12},{9,13},{10,... | collective-permute-start | bytes 172040 | tf_op jit(solution)/shard_map/ppermute | solution.py:136
  10.4 0.0 collective-permute-done.5.refs_3_.refs_1_
  10.4 0.0 collective-permute-done.1.refs_0_.refs_1_
  10.4 0.9 %shard_map.58.refs_2_ = f32[8,416]{1,0:T(8,128)S(1)} custom-call(bf16[2,112,128]{2,1,0:T(8,128)(2,1)S(1)} %pad_maximum_fusion.refs_0_, bf16[2,112,128]{2,1,0:T(8,128)(2,1)S(1)} %collective-permute-done.1.refs_0_.refs_1_, bf16[2,112,128]{2,1,0:T(8,128)(2,1)S(1)} %constant_dynamic-update-slice_fusion.refs_1_.refs_2_, ...), custom_call_target="tpu_custom_call" | custom-call | flops 21265121280 | tf_op jit(solution)/shard_map/pallas_call | solution.py:122
  11.3 0.0 collective-permute-done.4.refs_2_.refs_0_
  11.3 0.6 %shard_map.59 = f32[8,416]{1,0:T(8,128)S(1)} custom-call(bf16[2,112,128]{2,1,0:T(8,128)(2,1)S(1)} %collective-permute-done.4.refs_2_.refs_0_, bf16[32,416]{1,0:T(8,128)(2,1)S(1)} %collective-permute-done.5.refs_3_.refs_1_, f32[8,416]{1,0:T(8,128)S(1)} %shard_map.58.refs_2_), custom_call_target="tpu_custom_call" | custom-call | flops 7088373760 | tf_op jit(solution)/shard_map/pallas_call | solution.py:122
  11.9 1.4 %collective-permute-start.6 = (f32[8,416]{1,0:T(8,128)S(1)}, f32[8,416]{1,0:T(8,128)S(1)}, u32[]{:S(2)}, u32[]{:S(2)}) collective-permute-start(f32[8,416]{1,0:T(8,128)S(1)} %shard_map.59), channel_id=1, source_target_pairs={{0,12},{1,13},{2,14},{3,15},{4,8},{5,9},{6,10},{7,11},{8,4},{9,5},... | collective-permute-start | bytes 39944 | tf_op jit(solution)/shard_map/ppermute | solution.py:136
  13.3 0.9 %shard_map.57 = f32[8,416]{1,0:T(8,128)S(1)} custom-call(bf16[2,112,128]{2,1,0:T(8,128)(2,1)S(1)} %collective-permute-done.1.refs_0_.refs_1_, bf16[2,112,128]{2,1,0:T(8,128)(2,1)S(1)} %constant_dynamic-update-slice_fusion.refs_1_.refs_2_, bf16[2,112,128]{2,1,0:T(8,128)(2,1)S(1)} %collective-permute-done.4.refs_2_.refs_0_, ...), custom_call_target="tpu_custom_call" | custom-call | flops 21265121280 | tf_op jit(solution)/shard_map/pallas_call | solution.py:122
  14.3 0.9 %collective-permute-done.6 = f32[8,416]{1,0:T(8,128)S(1)} collective-permute-done((f32[8,416]{1,0:T(8,128)S(1)}, f32[8,416]{1,0:T(8,128)S(1)}, u32[]{:S(2)}, u32[]{:S(2)}) %collective-permute-start.6) | collective-permute-done | bytes 13344 | tf_op jit(solution)/shard_map/ppermute | solution.py:136
  15.2 0.6 %add.3 = f32[8,416]{1,0:T(8,128)} add(f32[8,416]{1,0:T(8,128)S(1)} %shard_map.57, f32[8,416]{1,0:T(8,128)S(1)} %collective-permute-done.6) | non-fusion elementwise | flops 3328 | bytes 39936 | tf_op jit(solution)/shard_map/add | solution.py:177
  (3 shorter events, 0.0 us)
Async XLA Ops:
  1.0 6.8 %collective-permute-start = (bf16[1,112,128]{2,1,0:T(8,128)(2,1)S(1)}, bf16[1,112,128]{2,1,0:T(8,128)(2,1)S(1)}, u32[]{:S(2)}, u32[]{:S(2)}) collective-permute-start(bf16[1,112,128]{2,1,0:T(8,128)(2,1)S(1)} %bitcast.4), channel_id=1, source_target_pairs={{0,7},{1,6},{2,5},{3,4},{4,3},{5,2},{6,1},{7,0},{8,15},{9,14},{10,... | collective-permute-start | bytes 86024 | tf_op jit(solution)/shard_map/ppermute | solution.py:136
  5.5 4.5 %collective-permute-start.3 = (bf16[1,112,128]{2,1,0:T(8,128)(2,1)S(1)}, bf16[1,112,128]{2,1,0:T(8,128)(2,1)S(1)}, u32[]{:S(2)}, u32[]{:S(2)}) collective-permute-start(bf16[1,112,128]{2,1,0:T(8,128)(2,1)S(1)} %bitcast.5), channel_id=1, source_target_pairs={{0,6},{1,7},{2,4},{3,5},{4,2},{5,3},{6,0},{7,1},{8,14},{9,15},{10,... | collective-permute-start | bytes 86024 | tf_op jit(solution)/shard_map/ppermute | solution.py:136
  5.5 3.3 %collective-permute-start.2 = (bf16[1,112,128]{2,1,0:T(8,128)(2,1)S(1)}, bf16[1,112,128]{2,1,0:T(8,128)(2,1)S(1)}, u32[]{:S(2)}, u32[]{:S(2)}) collective-permute-start(bf16[1,112,128]{2,1,0:T(8,128)(2,1)S(1)} %bitcast.6), channel_id=1, source_target_pairs={{0,5},{1,4},{2,7},{3,6},{4,1},{5,0},{6,3},{7,2},{8,13},{9,12},{10,... | collective-permute-start | bytes 86024 | tf_op jit(solution)/shard_map/ppermute | solution.py:136
  6.4 4.0 %collective-permute-start.5 = (bf16[32,416]{1,0:T(8,128)(2,1)S(1)}, bf16[32,416]{1,0:T(8,128)(2,1)S(1)}, u32[]{:S(2)}, u32[]{:S(2)}) collective-permute-start(bf16[32,416]{1,0:T(8,128)(2,1)S(1)} %get-tuple-element.11.refs_1_.refs_3_), channel_id=1, source_target_pairs={{0,12},{1,13},{2,14},{3,15},{4,8},{5,9},{6,10},{7,11},{8,4},{9,5},... | collective-permute-start | bytes 79880 | tf_op jit(solution)/shard_map/ppermute | solution.py:136
  8.3 2.1 %collective-permute-start.1 = (bf16[2,112,128]{2,1,0:T(8,128)(2,1)S(1)}, bf16[2,112,128]{2,1,0:T(8,128)(2,1)S(1)}, u32[]{:S(2)}, u32[]{:S(2)}) collective-permute-start(bf16[2,112,128]{2,1,0:T(8,128)(2,1)S(1)} %pad_maximum_fusion.refs_0_), channel_id=1, source_target_pairs={{0,4},{1,5},{2,6},{3,7},{4,0},{5,1},{6,2},{7,3},{8,12},{9,13},{10,... | collective-permute-start | bytes 172040 | tf_op jit(solution)/shard_map/ppermute | solution.py:136
  10.0 1.4 %collective-permute-start.4 = (bf16[2,112,128]{2,1,0:T(8,128)(2,1)S(1)}, bf16[2,112,128]{2,1,0:T(8,128)(2,1)S(1)}, u32[]{:S(2)}, u32[]{:S(2)}) collective-permute-start(bf16[2,112,128]{2,1,0:T(8,128)(2,1)S(1)} %constant_dynamic-update-slice_fusion.refs_1_.refs_2_), channel_id=1, source_target_pairs={{0,4},{1,5},{2,6},{3,7},{4,0},{5,1},{6,2},{7,3},{8,12},{9,13},{10,... | collective-permute-start | bytes 172040 | tf_op jit(solution)/shard_map/ppermute | solution.py:136
  11.9 3.3 %collective-permute-start.6 = (f32[8,416]{1,0:T(8,128)S(1)}, f32[8,416]{1,0:T(8,128)S(1)}, u32[]{:S(2)}, u32[]{:S(2)}) collective-permute-start(f32[8,416]{1,0:T(8,128)S(1)} %shard_map.59), channel_id=1, source_target_pairs={{0,12},{1,13},{2,14},{3,15},{4,8},{5,9},{6,10},{7,11},{8,4},{9,5},... | collective-permute-start | bytes 39944 | tf_op jit(solution)/shard_map/ppermute | solution.py:136

commit v6 on v5

--- a/solution.py
+++ b/solution.py
@@ -132,6 +132,14 @@
     rows, cols = mesh_shape
     pairs = [
         (r * cols + c, (r ^ row_bits) * cols + (c ^ col_bits)) for r in range(rows) for c in range(cols)
+    ]
+    return lax.ppermute(x, ("rows", "cols"), pairs)
+
+
+def turn(x, mesh_shape, row_bits, places):
+    rows, cols = mesh_shape
+    pairs = [
+        (r * cols + c, (r ^ row_bits) * cols + c // 4 * 4 + places[c % 4]) for r in range(rows) for c in range(cols)
     ]
     return lax.ppermute(x, ("rows", "cols"), pairs)
 
@@ -164,9 +172,11 @@
     for step in [(1, bits) for bits in powers(cols)[:-2]] + [(bits + 1, 0) for bits in powers(rows)[:-2]]:
         one = jnp.concatenate([one, swap(one, mesh_shape, *step)], axis=0)
     peer = swap(block, mesh_shape, 3, 0)
-    next_to, second, far = (swap(one, mesh_shape, 1, bits) for bits in (1, 2, 3))
-    early = jnp.concatenate([one, far], axis=0)
-    late = jnp.concatenate([next_to, second], axis=0)
+    next_to = swap(one, mesh_shape, 1, 1)
+    ahead = turn(one, mesh_shape, 0, (2, 3, 1, 0))
+    behind = turn(one, mesh_shape, 1, (3, 2, 0, 1))
+    early = jnp.concatenate([one, ahead], axis=0)
+    late = jnp.concatenate([next_to, behind], axis=0)
     total = add(features, [early], block, base)
     sent, total = lax.optimization_barrier((early, total))
     early_other = swap(sent, mesh_shape, 1, 0)

time: 16 us -> 15.4 us (0.963)
  starting transfers between devices: 8.99 us -> 8.67 us
  waiting for transfers between devices: 2.21 us -> 2.04 us
    ppermute x7 -> x5, starting transfers between devices: 8.99 us -> 4.12 us  [swap(): return lax.ppermute(x, ('rows', 'cols'), pairs)]
    ppermute x0 -> x2, starting transfers between devices: none -> 4.55 us  [turn(): return lax.ppermute(x, ('rows', 'cols'), pairs)]
    ppermute x7 -> x5, waiting for transfers between devices: 2.21 us -> 2 us  [swap(): return lax.ppermute(x, ('rows', 'cols'), pairs)]
  transfers between devices with their start and end apart: 7 -> 7, of which waited for: 3 -> 3; matrix products, arithmetic and copies ran while one was open for 0% -> 0% of each run, Pallas kernels for 15% -> 16%
where the time goes in v6:
time: 15.4 us; the launch traced here: 15.2 us
  starting transfers between devices  8.67 us (56%)
  Pallas kernels  3.82 us (25%)
  waiting for transfers between devices  2.04 us (13%)
  other arithmetic  0.62 us (4%)
    ppermute x2, starting transfers between devices, turn(): return lax.ppermute(x, ('rows', 'cols'), pairs)  4.55 us
    ppermute x5, starting transfers between devices, swap(): return lax.ppermute(x, ('rows', 'cols'), pairs)  4.12 us
    pallas_call x4, Pallas kernels, add(): pl.pallas_call(functools.partial(add_blocks, features, counts), out_shape...  2.83 us
    ppermute x5, waiting for transfers between devices, swap(): return lax.ppermute(x, ('rows', 'cols'), pairs)  2 us
    pallas_call x1, Pallas kernels, local(): pl.pallas_call(prepare_kernel, out_shape=(VMEM((height, width), jnp.bfloa...  0.99 us
    add x1, other arithmetic, local(): return total + swap(partial, mesh_shape, 3, 0)  0.61 us
  transfers between devices with their start and end apart: 7, of which 3 were waited for; matrix products, arithmetic and copies ran while one was open for 0% of the time, Pallas kernels for 16%

profile of v6, /device:TPU:0, one launch (start us, length us, event | category | flops | bytes accessed | tf_op | source)
XLA Modules:
  0.0 15.2 jit_solution(13421027861421637368)
XLA Ops:
  0.0 1.0 %shard_map.55 = (bf16[32,416]{1,0:T(8,128)(2,1)S(1)}, f32[8,416]{1,0:T(8,128)S(1)}, bf16[112,128]{1,0:T(8,128)(2,1)S(1)}) custom-call(f32[24,416]{1,0:T(8,128)} %points_ref.1, f32[1,24]{1,0:T(1,128)} %bitcast.10, f32[1,416]{1,0:T(1,128)} %bitcast.8, s32[7,416]{1,0:T(8,128)} %probes_ref.1, f32[1,416]{1,0:T(1,128)} %bitcast.9), custom_call_target="tpu_custom_call" | custom-call | tf_op jit(solution)/shard_map/pallas_call | solution.py:161
  1.0 4.0 %collective-permute-start = (bf16[1,112,128]{2,1,0:T(8,128)(2,1)S(1)}, bf16[1,112,128]{2,1,0:T(8,128)(2,1)S(1)}, u32[]{:S(2)}, u32[]{:S(2)}) collective-permute-start(bf16[1,112,128]{2,1,0:T(8,128)(2,1)S(1)} %bitcast.4), channel_id=1, source_target_pairs={{0,2},{1,3},{2,1},{3,0},{4,6},{5,7},{6,5},{7,4},{8,10},{9,11},{10,... | collective-permute-start | bytes 86024 | tf_op jit(solution)/shard_map/ppermute | solution.py:144
  5.0 0.5 %collective-permute-start.3 = (bf16[1,112,128]{2,1,0:T(8,128)(2,1)S(1)}, bf16[1,112,128]{2,1,0:T(8,128)(2,1)S(1)}, u32[]{:S(2)}, u32[]{:S(2)}) collective-permute-start(bf16[1,112,128]{2,1,0:T(8,128)(2,1)S(1)} %bitcast.5), channel_id=1, source_target_pairs={{0,7},{1,6},{2,4},{3,5},{4,3},{5,2},{6,0},{7,1},{8,15},{9,14},{10,... | collective-permute-start | bytes 86024 | tf_op jit(solution)/shard_map/ppermute | solution.py:144
  5.5 0.2 %collective-permute-start.2 = (bf16[1,112,128]{2,1,0:T(8,128)(2,1)S(1)}, bf16[1,112,128]{2,1,0:T(8,128)(2,1)S(1)}, u32[]{:S(2)}, u32[]{:S(2)}) collective-permute-start(bf16[1,112,128]{2,1,0:T(8,128)(2,1)S(1)} %bitcast.6), channel_id=1, source_target_pairs={{0,5},{1,4},{2,7},{3,6},{4,1},{5,0},{6,3},{7,2},{8,13},{9,12},{10,... | collective-permute-start | bytes 86024 | tf_op jit(solution)/shard_map/ppermute | solution.py:136
  5.8 2.1 %collective-permute-start.5 = (bf16[32,416]{1,0:T(8,128)(2,1)S(1)}, bf16[32,416]{1,0:T(8,128)(2,1)S(1)}, u32[]{:S(2)}, u32[]{:S(2)}) collective-permute-start(bf16[32,416]{1,0:T(8,128)(2,1)S(1)} %get-tuple-element.11.refs_1_.refs_3_), channel_id=1, source_target_pairs={{0,12},{1,13},{2,14},{3,15},{4,8},{5,9},{6,10},{7,11},{8,4},{9,5},... | collective-permute-start | bytes 79880 | tf_op jit(solution)/shard_map/ppermute | solution.py:136
  7.9 0.0 collective-permute-done
  7.9 0.5 %shard_map.56.refs_4_ = f32[8,416]{1,0:T(8,128)S(1)} custom-call(bf16[2,112,128]{2,1,0:T(8,128)(2,1)S(1)} %pad_maximum_fusion.refs_0_, bf16[32,416]{1,0:T(8,128)(2,1)S(1)} %get-tuple-element.11.refs_1_.refs_3_, f32[8,416]{1,0:T(8,128)S(1)} %get-tuple-element.12.refs_2_), custom_call_target="tpu_custom_call" | custom-call | flops 7088373760 | tf_op jit(solution)/shard_map/pallas_call | solution.py:122
  8.4 0.1 collective-permute-start.1
  8.5 1.1 %collective-permute-done.2 = bf16[1,112,128]{2,1,0:T(8,128)(2,1)S(1)} collective-permute-done((bf16[1,112,128]{2,1,0:T(8,128)(2,1)S(1)}, bf16[1,112,128]{2,1,0:T(8,128)(2,1)S(1)}, u32[]{:S(2)}, u32[]{:S(2)}) %collective-permute-start.2) | collective-permute-done | bytes 28704 | tf_op jit(solution)/shard_map/ppermute | solution.py:136
  9.5 0.0 collective-permute-done.3
  9.5 0.2 %collective-permute-start.4 = (bf16[2,112,128]{2,1,0:T(8,128)(2,1)S(1)}, bf16[2,112,128]{2,1,0:T(8,128)(2,1)S(1)}, u32[]{:S(2)}, u32[]{:S(2)}) collective-permute-start(bf16[2,112,128]{2,1,0:T(8,128)(2,1)S(1)} %constant_dynamic-update-slice_fusion.refs_1_.refs_2_), channel_id=1, source_target_pairs={{0,4},{1,5},{2,6},{3,7},{4,0},{5,1},{6,2},{7,3},{8,12},{9,13},{10,... | collective-permute-start | bytes 172040 | tf_op jit(solution)/shard_map/ppermute | solution.py:136
  9.7 0.0 collective-permute-done.5.refs_3_.refs_1_
  9.7 0.0 collective-permute-done.1.refs_0_.refs_1_
  9.7 0.9 %shard_map.58.refs_2_ = f32[8,416]{1,0:T(8,128)S(1)} custom-call(bf16[2,112,128]{2,1,0:T(8,128)(2,1)S(1)} %pad_maximum_fusion.refs_0_, bf16[2,112,128]{2,1,0:T(8,128)(2,1)S(1)} %collective-permute-done.1.refs_0_.refs_1_, bf16[2,112,128]{2,1,0:T(8,128)(2,1)S(1)} %constant_dynamic-update-slice_fusion.refs_1_.refs_2_, ...), custom_call_target="tpu_custom_call" | custom-call | flops 21265121280 | tf_op jit(solution)/shard_map/pallas_call | solution.py:122
  10.7 0.2 %collective-permute-done.4.refs_2_.refs_0_ = bf16[2,112,128]{2,1,0:T(8,128)(2,1)S(1)} collective-permute-done((bf16[2,112,128]{2,1,0:T(8,128)(2,1)S(1)}, bf16[2,112,128]{2,1,0:T(8,128)(2,1)S(1)}, u32[]{:S(2)}, u32[]{:S(2)}) %collective-permute-start.4) | collective-permute-done | bytes 57376 | tf_op jit(solution)/shard_map/ppermute | solution.py:136
  10.8 0.5 %shard_map.59 = f32[8,416]{1,0:T(8,128)S(1)} custom-call(bf16[2,112,128]{2,1,0:T(8,128)(2,1)S(1)} %collective-permute-done.4.refs_2_.refs_0_, bf16[32,416]{1,0:T(8,128)(2,1)S(1)} %collective-permute-done.5.refs_3_.refs_1_, f32[8,416]{1,0:T(8,128)S(1)} %shard_map.58.refs_2_), custom_call_target="tpu_custom_call" | custom-call | flops 7088373760 | tf_op jit(solution)/shard_map/pallas_call | solution.py:122
  11.3 1.6 %collective-permute-start.6 = (f32[8,416]{1,0:T(8,128)S(1)}, f32[8,416]{1,0:T(8,128)S(1)}, u32[]{:S(2)}, u32[]{:S(2)}) collective-permute-start(f32[8,416]{1,0:T(8,128)S(1)} %shard_map.59), channel_id=1, source_target_pairs={{0,12},{1,13},{2,14},{3,15},{4,8},{5,9},{6,10},{7,11},{8,4},{9,5},... | collective-permute-start | bytes 39944 | tf_op jit(solution)/shard_map/ppermute | solution.py:136
  12.9 0.9 %shard_map.57 = f32[8,416]{1,0:T(8,128)S(1)} custom-call(bf16[2,112,128]{2,1,0:T(8,128)(2,1)S(1)} %collective-permute-done.1.refs_0_.refs_1_, bf16[2,112,128]{2,1,0:T(8,128)(2,1)S(1)} %constant_dynamic-update-slice_fusion.refs_1_.refs_2_, bf16[2,112,128]{2,1,0:T(8,128)(2,1)S(1)} %collective-permute-done.4.refs_2_.refs_0_, ...), custom_call_target="tpu_custom_call" | custom-call | flops 21265121280 | tf_op jit(solution)/shard_map/pallas_call | solution.py:122
  13.8 0.8 %collective-permute-done.6 = f32[8,416]{1,0:T(8,128)S(1)} collective-permute-done((f32[8,416]{1,0:T(8,128)S(1)}, f32[8,416]{1,0:T(8,128)S(1)}, u32[]{:S(2)}, u32[]{:S(2)}) %collective-permute-start.6) | collective-permute-done | bytes 13344 | tf_op jit(solution)/shard_map/ppermute | solution.py:136
  14.6 0.6 %add.3 = f32[8,416]{1,0:T(8,128)} add(f32[8,416]{1,0:T(8,128)S(1)} %shard_map.57, f32[8,416]{1,0:T(8,128)S(1)} %collective-permute-done.6) | non-fusion elementwise | flops 3328 | bytes 39936 | tf_op jit(solution)/shard_map/add | solution.py:187
  (3 shorter events, 0.0 us)
Async XLA Ops:
  1.0 6.9 %collective-permute-start = (bf16[1,112,128]{2,1,0:T(8,128)(2,1)S(1)}, bf16[1,112,128]{2,1,0:T(8,128)(2,1)S(1)}, u32[]{:S(2)}, u32[]{:S(2)}) collective-permute-start(bf16[1,112,128]{2,1,0:T(8,128)(2,1)S(1)} %bitcast.4), channel_id=1, source_target_pairs={{0,2},{1,3},{2,1},{3,0},{4,6},{5,7},{6,5},{7,4},{8,10},{9,11},{10,... | collective-permute-start | bytes 86024 | tf_op jit(solution)/shard_map/ppermute | solution.py:144
  5.0 4.5 %collective-permute-start.3 = (bf16[1,112,128]{2,1,0:T(8,128)(2,1)S(1)}, bf16[1,112,128]{2,1,0:T(8,128)(2,1)S(1)}, u32[]{:S(2)}, u32[]{:S(2)}) collective-permute-start(bf16[1,112,128]{2,1,0:T(8,128)(2,1)S(1)} %bitcast.5), channel_id=1, source_target_pairs={{0,7},{1,6},{2,4},{3,5},{4,3},{5,2},{6,0},{7,1},{8,15},{9,14},{10,... | collective-permute-start | bytes 86024 | tf_op jit(solution)/shard_map/ppermute | solution.py:144
  5.5 4.0 %collective-permute-start.2 = (bf16[1,112,128]{2,1,0:T(8,128)(2,1)S(1)}, bf16[1,112,128]{2,1,0:T(8,128)(2,1)S(1)}, u32[]{:S(2)}, u32[]{:S(2)}) collective-permute-start(bf16[1,112,128]{2,1,0:T(8,128)(2,1)S(1)} %bitcast.6), channel_id=1, source_target_pairs={{0,5},{1,4},{2,7},{3,6},{4,1},{5,0},{6,3},{7,2},{8,13},{9,12},{10,... | collective-permute-start | bytes 86024 | tf_op jit(solution)/shard_map/ppermute | solution.py:136
  5.8 3.9 %collective-permute-start.5 = (bf16[32,416]{1,0:T(8,128)(2,1)S(1)}, bf16[32,416]{1,0:T(8,128)(2,1)S(1)}, u32[]{:S(2)}, u32[]{:S(2)}) collective-permute-start(bf16[32,416]{1,0:T(8,128)(2,1)S(1)} %get-tuple-element.11.refs_1_.refs_3_), channel_id=1, source_target_pairs={{0,12},{1,13},{2,14},{3,15},{4,8},{5,9},{6,10},{7,11},{8,4},{9,5},... | collective-permute-start | bytes 79880 | tf_op jit(solution)/shard_map/ppermute | solution.py:136
  8.4 1.4 %collective-permute-start.1 = (bf16[2,112,128]{2,1,0:T(8,128)(2,1)S(1)}, bf16[2,112,128]{2,1,0:T(8,128)(2,1)S(1)}, u32[]{:S(2)}, u32[]{:S(2)}) collective-permute-start(bf16[2,112,128]{2,1,0:T(8,128)(2,1)S(1)} %pad_maximum_fusion.refs_0_), channel_id=1, source_target_pairs={{0,4},{1,5},{2,6},{3,7},{4,0},{5,1},{6,2},{7,3},{8,12},{9,13},{10,... | collective-permute-start | bytes 172040 | tf_op jit(solution)/shard_map/ppermute | solution.py:136
  9.5 1.3 %collective-permute-start.4 = (bf16[2,112,128]{2,1,0:T(8,128)(2,1)S(1)}, bf16[2,112,128]{2,1,0:T(8,128)(2,1)S(1)}, u32[]{:S(2)}, u32[]{:S(2)}) collective-permute-start(bf16[2,112,128]{2,1,0:T(8,128)(2,1)S(1)} %constant_dynamic-update-slice_fusion.refs_1_.refs_2_), channel_id=1, source_target_pairs={{0,4},{1,5},{2,6},{3,7},{4,0},{5,1},{6,2},{7,3},{8,12},{9,13},{10,... | collective-permute-start | bytes 172040 | tf_op jit(solution)/shard_map/ppermute | solution.py:136
  11.3 3.3 %collective-permute-start.6 = (f32[8,416]{1,0:T(8,128)S(1)}, f32[8,416]{1,0:T(8,128)S(1)}, u32[]{:S(2)}, u32[]{:S(2)}) collective-permute-start(f32[8,416]{1,0:T(8,128)S(1)} %shard_map.59), channel_id=1, source_target_pairs={{0,12},{1,13},{2,14},{3,15},{4,8},{5,9},{6,10},{7,11},{8,4},{9,5},... | collective-permute-start | bytes 39944 | tf_op jit(solution)/shard_map/ppermute | solution.py:136

commit v7 on v6

--- a/solution.py
+++ b/solution.py
@@ -18,7 +18,7 @@
     return pltpu.with_memory_space_constraint(x, VMEM)
 
 
-def prepare_kernel(points_ref, lengthscale_ref, target_ref, probes_ref, noise_ref, block_ref, base_ref, packed_ref):
+def prepare_kernel(points_ref, lengthscale_ref, target_ref, probes_ref, noise_ref, scaled_ref, base_ref, packed_ref):
     features = points_ref.shape[0]
     wide = jnp.broadcast_to(lengthscale_ref[...], (features, features))
     row = lax.broadcasted_iota(jnp.int32, wide.shape, 0)
@@ -34,12 +34,14 @@
     high, low = block[: rows // 2, full:], block[rows // 2 :, full:]
     packed_ref[full // LANES * rows :, :] = jnp.concatenate([high, low, high, low], axis=1).astype(jnp.bfloat16)
     block = block.astype(jnp.bfloat16)
-    block_ref[...] = block
+    scaled_ref[...] = block[:features]
     base_ref[...] = noise_ref[...] * block[features:].astype(jnp.float32)
 
 
 def augmented(block, features, own):
     x = block.astype(jnp.float32)
+    if own:
+        x = jnp.concatenate([x, jnp.zeros((8, x.shape[1]), jnp.float32)], axis=0)
     row = lax.broadcasted_iota(jnp.int32, x.shape, 0)
     x = jnp.where(row < features, x, 0.0)
     half = -0.5 * jnp.sum(x * x, axis=0, keepdims=True)
@@ -78,7 +80,7 @@
     own_ref, out_ref = refs[len(counts)], refs[-1]
     total = refs[len(counts) + 1][...] if len(refs) == len(counts) + 3 else None
     own_side = augmented(own_ref[...], features, True)
-    rows = own_ref.shape[0]
+    rows = features + out_ref.shape[0]
     low = features // 16 * 16
     blocks = [(ref, k) for ref, count in zip(piece_refs, counts) for k in range(count)]
     whole = piece_refs[0].shape[1] // rows * rows
@@ -112,11 +114,11 @@
     out_ref[...] = found
 
 
-def add(features, pieces, own, total=None):
-    rows, width = own.shape
+def add(vectors, pieces, own, total=None):
+    features, width = own.shape
     counts = tuple(piece.shape[0] for piece in pieces)
     operands = [near(x) for x in (*pieces, own, total) if x is not None]
-    shape = (rows - features, width)
+    shape = (vectors, width)
     out = VMEM(shape, jnp.float32)
     work = sum(counts) * width * width
     return pl.pallas_call(
@@ -158,10 +160,10 @@
     vectors = probes.shape[0] + 1
     height = features + vectors
     packed_rows = width // LANES * height + height // 2
-    block, base, packed = pl.pallas_call(
+    scaled, base, packed = pl.pallas_call(
         prepare_kernel,
         out_shape=(
-            VMEM((height, width), jnp.bfloat16),
+            VMEM((features, width), jnp.bfloat16),
             VMEM((vectors, width), jnp.float32),
             VMEM((packed_rows, LANES), jnp.bfloat16),
         ),
@@ -171,19 +173,19 @@
     one = packed[None]
     for step in [(1, bits) for bits in powers(cols)[:-2]] + [(bits + 1, 0) for bits in powers(rows)[:-2]]:
         one = jnp.concatenate([one, swap(one, mesh_shape, *step)], axis=0)
-    peer = swap(block, mesh_shape, 3, 0)
+    peer = swap(scaled, mesh_shape, 3, 0)
     next_to = swap(one, mesh_shape, 1, 1)
     ahead = turn(one, mesh_shape, 0, (2, 3, 1, 0))
     behind = turn(one, mesh_shape, 1, (3, 2, 0, 1))
     early = jnp.concatenate([one, ahead], axis=0)
     late = jnp.concatenate([next_to, behind], axis=0)
-    total = add(features, [early], block, base)
+    total = add(vectors, [early], scaled, base)
     sent, total = lax.optimization_barrier((early, total))
     early_other = swap(sent, mesh_shape, 1, 0)
     late_other = swap(late, mesh_shape, 1, 0)
-    partial = add(features, [early, early_other, late], peer)
-    partial = add(features, [late_other], peer, partial)
-    total = add(features, [early_other, late, late_other], block, total)
+    partial = add(vectors, [early, early_other, late], peer)
+    partial = add(vectors, [late_other], peer, partial)
+    total = add(vectors, [early_other, late, late_other], scaled, total)
     return total + swap(partial, mesh_shape, 3, 0)
 
 

time: 15.4 us -> 15.4 us (level)
  no operation moved by 1% of the time
where the time goes in v7:
time: 15.4 us; the launch traced here: 15.2 us
  starting transfers between devices  8.67 us (56%)
  Pallas kernels  3.82 us (25%)
  waiting for transfers between devices  2.04 us (13%)
  other arithmetic  0.62 us (4%)
    ppermute x2, starting transfers between devices, turn(): return lax.ppermute(x, ('rows', 'cols'), pairs)  4.55 us
    ppermute x5, starting transfers between devices, swap(): return lax.ppermute(x, ('rows', 'cols'), pairs)  4.12 us
    pallas_call x4, Pallas kernels, add(): pl.pallas_call(functools.partial(add_blocks, features, counts), out_shape...  2.83 us
    ppermute x5, waiting for transfers between devices, swap(): return lax.ppermute(x, ('rows', 'cols'), pairs)  2 us
    pallas_call x1, Pallas kernels, local(): pl.pallas_call(prepare_kernel, out_shape=(VMEM((features, width), jnp.bfl...  0.99 us
    add x1, other arithmetic, local(): return total + swap(partial, mesh_shape, 3, 0)  0.61 us
  transfers between devices with their start and end apart: 7, of which 3 were waited for; matrix products, arithmetic and copies ran while one was open for 0% of the time, Pallas kernels for 16%

profile of v7, /device:TPU:0, one launch (start us, length us, event | category | flops | bytes accessed | tf_op | source)
XLA Modules:
  0.0 15.2 jit_solution(11370211939791248390)
XLA Ops:
  0.0 1.0 %shard_map.55 = (bf16[24,416]{1,0:T(8,128)(2,1)S(1)}, f32[8,416]{1,0:T(8,128)S(1)}, bf16[112,128]{1,0:T(8,128)(2,1)S(1)}) custom-call(f32[24,416]{1,0:T(8,128)} %points_ref.1, f32[1,24]{1,0:T(1,128)} %bitcast.10, f32[1,416]{1,0:T(1,128)} %bitcast.8, s32[7,416]{1,0:T(8,128)} %probes_ref.1, f32[1,416]{1,0:T(1,128)} %bitcast.9), custom_call_target="tpu_custom_call" | custom-call | tf_op jit(solution)/shard_map/pallas_call | solution.py:163
  1.0 4.0 %collective-permute-start = (bf16[1,112,128]{2,1,0:T(8,128)(2,1)S(1)}, bf16[1,112,128]{2,1,0:T(8,128)(2,1)S(1)}, u32[]{:S(2)}, u32[]{:S(2)}) collective-permute-start(bf16[1,112,128]{2,1,0:T(8,128)(2,1)S(1)} %bitcast.4), channel_id=1, source_target_pairs={{0,2},{1,3},{2,1},{3,0},{4,6},{5,7},{6,5},{7,4},{8,10},{9,11},{10,... | collective-permute-start | bytes 86024 | tf_op jit(solution)/shard_map/ppermute | solution.py:146
  5.0 0.5 %collective-permute-start.3 = (bf16[1,112,128]{2,1,0:T(8,128)(2,1)S(1)}, bf16[1,112,128]{2,1,0:T(8,128)(2,1)S(1)}, u32[]{:S(2)}, u32[]{:S(2)}) collective-permute-start(bf16[1,112,128]{2,1,0:T(8,128)(2,1)S(1)} %bitcast.5), channel_id=1, source_target_pairs={{0,7},{1,6},{2,4},{3,5},{4,3},{5,2},{6,0},{7,1},{8,15},{9,14},{10,... | collective-permute-start | bytes 86024 | tf_op jit(solution)/shard_map/ppermute | solution.py:146
  5.5 0.2 %collective-permute-start.2 = (bf16[1,112,128]{2,1,0:T(8,128)(2,1)S(1)}, bf16[1,112,128]{2,1,0:T(8,128)(2,1)S(1)}, u32[]{:S(2)}, u32[]{:S(2)}) collective-permute-start(bf16[1,112,128]{2,1,0:T(8,128)(2,1)S(1)} %bitcast.6), channel_id=1, source_target_pairs={{0,5},{1,4},{2,7},{3,6},{4,1},{5,0},{6,3},{7,2},{8,13},{9,12},{10,... | collective-permute-start | bytes 86024 | tf_op jit(solution)/shard_map/ppermute | solution.py:138
  5.8 2.1 %collective-permute-start.5 = (bf16[24,416]{1,0:T(8,128)(2,1)S(1)}, bf16[24,416]{1,0:T(8,128)(2,1)S(1)}, u32[]{:S(2)}, u32[]{:S(2)}) collective-permute-start(bf16[24,416]{1,0:T(8,128)(2,1)S(1)} %get-tuple-element.11.refs_1_.refs_3_), channel_id=1, source_target_pairs={{0,12},{1,13},{2,14},{3,15},{4,8},{5,9},{6,10},{7,11},{8,4},{9,5},... | collective-permute-start | bytes 59912 | tf_op jit(solution)/shard_map/ppermute | solution.py:138
  7.9 0.0 collective-permute-done
  7.9 0.5 %shard_map.56.refs_4_ = f32[8,416]{1,0:T(8,128)S(1)} custom-call(bf16[2,112,128]{2,1,0:T(8,128)(2,1)S(1)} %pad_maximum_fusion.refs_0_, bf16[24,416]{1,0:T(8,128)(2,1)S(1)} %get-tuple-element.11.refs_1_.refs_3_, f32[8,416]{1,0:T(8,128)S(1)} %get-tuple-element.12.refs_2_), custom_call_target="tpu_custom_call" | custom-call | flops 7088373760 | tf_op jit(solution)/shard_map/pallas_call | solution.py:124
  8.4 0.1 collective-permute-start.1
  8.5 1.1 %collective-permute-done.2 = bf16[1,112,128]{2,1,0:T(8,128)(2,1)S(1)} collective-permute-done((bf16[1,112,128]{2,1,0:T(8,128)(2,1)S(1)}, bf16[1,112,128]{2,1,0:T(8,128)(2,1)S(1)}, u32[]{:S(2)}, u32[]{:S(2)}) %collective-permute-start.2) | collective-permute-done | bytes 28704 | tf_op jit(solution)/shard_map/ppermute | solution.py:138
  9.5 0.0 collective-permute-done.3
  9.5 0.2 %collective-permute-start.4 = (bf16[2,112,128]{2,1,0:T(8,128)(2,1)S(1)}, bf16[2,112,128]{2,1,0:T(8,128)(2,1)S(1)}, u32[]{:S(2)}, u32[]{:S(2)}) collective-permute-start(bf16[2,112,128]{2,1,0:T(8,128)(2,1)S(1)} %constant_dynamic-update-slice_fusion.refs_1_.refs_2_), channel_id=1, source_target_pairs={{0,4},{1,5},{2,6},{3,7},{4,0},{5,1},{6,2},{7,3},{8,12},{9,13},{10,... | collective-permute-start | bytes 172040 | tf_op jit(solution)/shard_map/ppermute | solution.py:138
  9.7 0.0 collective-permute-done.5.refs_3_.refs_1_
  9.7 0.0 collective-permute-done.1.refs_0_.refs_1_
  9.7 0.9 %shard_map.58.refs_2_ = f32[8,416]{1,0:T(8,128)S(1)} custom-call(bf16[2,112,128]{2,1,0:T(8,128)(2,1)S(1)} %pad_maximum_fusion.refs_0_, bf16[2,112,128]{2,1,0:T(8,128)(2,1)S(1)} %collective-permute-done.1.refs_0_.refs_1_, bf16[2,112,128]{2,1,0:T(8,128)(2,1)S(1)} %constant_dynamic-update-slice_fusion.refs_1_.refs_2_, ...), custom_call_target="tpu_custom_call" | custom-call | flops 21265121280 | tf_op jit(solution)/shard_map/pallas_call | solution.py:124
  10.7 0.2 %collective-permute-done.4.refs_2_.refs_0_ = bf16[2,112,128]{2,1,0:T(8,128)(2,1)S(1)} collective-permute-done((bf16[2,112,128]{2,1,0:T(8,128)(2,1)S(1)}, bf16[2,112,128]{2,1,0:T(8,128)(2,1)S(1)}, u32[]{:S(2)}, u32[]{:S(2)}) %collective-permute-start.4) | collective-permute-done | bytes 57376 | tf_op jit(solution)/shard_map/ppermute | solution.py:138
  10.8 0.5 %shard_map.59 = f32[8,416]{1,0:T(8,128)S(1)} custom-call(bf16[2,112,128]{2,1,0:T(8,128)(2,1)S(1)} %collective-permute-done.4.refs_2_.refs_0_, bf16[24,416]{1,0:T(8,128)(2,1)S(1)} %collective-permute-done.5.refs_3_.refs_1_, f32[8,416]{1,0:T(8,128)S(1)} %shard_map.58.refs_2_), custom_call_target="tpu_custom_call" | custom-call | flops 7088373760 | tf_op jit(solution)/shard_map/pallas_call | solution.py:124
  11.3 1.6 %collective-permute-start.6 = (f32[8,416]{1,0:T(8,128)S(1)}, f32[8,416]{1,0:T(8,128)S(1)}, u32[]{:S(2)}, u32[]{:S(2)}) collective-permute-start(f32[8,416]{1,0:T(8,128)S(1)} %shard_map.59), channel_id=1, source_target_pairs={{0,12},{1,13},{2,14},{3,15},{4,8},{5,9},{6,10},{7,11},{8,4},{9,5},... | collective-permute-start | bytes 39944 | tf_op jit(solution)/shard_map/ppermute | solution.py:138
  12.9 0.9 %shard_map.57 = f32[8,416]{1,0:T(8,128)S(1)} custom-call(bf16[2,112,128]{2,1,0:T(8,128)(2,1)S(1)} %collective-permute-done.1.refs_0_.refs_1_, bf16[2,112,128]{2,1,0:T(8,128)(2,1)S(1)} %constant_dynamic-update-slice_fusion.refs_1_.refs_2_, bf16[2,112,128]{2,1,0:T(8,128)(2,1)S(1)} %collective-permute-done.4.refs_2_.refs_0_, ...), custom_call_target="tpu_custom_call" | custom-call | flops 21265121280 | tf_op jit(solution)/shard_map/pallas_call | solution.py:124
  13.8 0.8 %collective-permute-done.6 = f32[8,416]{1,0:T(8,128)S(1)} collective-permute-done((f32[8,416]{1,0:T(8,128)S(1)}, f32[8,416]{1,0:T(8,128)S(1)}, u32[]{:S(2)}, u32[]{:S(2)}) %collective-permute-start.6) | collective-permute-done | bytes 13344 | tf_op jit(solution)/shard_map/ppermute | solution.py:138
  14.6 0.6 %add.3 = f32[8,416]{1,0:T(8,128)} add(f32[8,416]{1,0:T(8,128)S(1)} %shard_map.57, f32[8,416]{1,0:T(8,128)S(1)} %collective-permute-done.6) | non-fusion elementwise | flops 3328 | bytes 39936 | tf_op jit(solution)/shard_map/add | solution.py:189
  (3 shorter events, 0.0 us)
Async XLA Ops:
  1.0 6.9 %collective-permute-start = (bf16[1,112,128]{2,1,0:T(8,128)(2,1)S(1)}, bf16[1,112,128]{2,1,0:T(8,128)(2,1)S(1)}, u32[]{:S(2)}, u32[]{:S(2)}) collective-permute-start(bf16[1,112,128]{2,1,0:T(8,128)(2,1)S(1)} %bitcast.4), channel_id=1, source_target_pairs={{0,2},{1,3},{2,1},{3,0},{4,6},{5,7},{6,5},{7,4},{8,10},{9,11},{10,... | collective-permute-start | bytes 86024 | tf_op jit(solution)/shard_map/ppermute | solution.py:146
  5.0 4.5 %collective-permute-start.3 = (bf16[1,112,128]{2,1,0:T(8,128)(2,1)S(1)}, bf16[1,112,128]{2,1,0:T(8,128)(2,1)S(1)}, u32[]{:S(2)}, u32[]{:S(2)}) collective-permute-start(bf16[1,112,128]{2,1,0:T(8,128)(2,1)S(1)} %bitcast.5), channel_id=1, source_target_pairs={{0,7},{1,6},{2,4},{3,5},{4,3},{5,2},{6,0},{7,1},{8,15},{9,14},{10,... | collective-permute-start | bytes 86024 | tf_op jit(solution)/shard_map/ppermute | solution.py:146
  5.5 4.0 %collective-permute-start.2 = (bf16[1,112,128]{2,1,0:T(8,128)(2,1)S(1)}, bf16[1,112,128]{2,1,0:T(8,128)(2,1)S(1)}, u32[]{:S(2)}, u32[]{:S(2)}) collective-permute-start(bf16[1,112,128]{2,1,0:T(8,128)(2,1)S(1)} %bitcast.6), channel_id=1, source_target_pairs={{0,5},{1,4},{2,7},{3,6},{4,1},{5,0},{6,3},{7,2},{8,13},{9,12},{10,... | collective-permute-start | bytes 86024 | tf_op jit(solution)/shard_map/ppermute | solution.py:138
  5.8 3.9 %collective-permute-start.5 = (bf16[24,416]{1,0:T(8,128)(2,1)S(1)}, bf16[24,416]{1,0:T(8,128)(2,1)S(1)}, u32[]{:S(2)}, u32[]{:S(2)}) collective-permute-start(bf16[24,416]{1,0:T(8,128)(2,1)S(1)} %get-tuple-element.11.refs_1_.refs_3_), channel_id=1, source_target_pairs={{0,12},{1,13},{2,14},{3,15},{4,8},{5,9},{6,10},{7,11},{8,4},{9,5},... | collective-permute-start | bytes 59912 | tf_op jit(solution)/shard_map/ppermute | solution.py:138
  8.4 1.4 %collective-permute-start.1 = (bf16[2,112,128]{2,1,0:T(8,128)(2,1)S(1)}, bf16[2,112,128]{2,1,0:T(8,128)(2,1)S(1)}, u32[]{:S(2)}, u32[]{:S(2)}) collective-permute-start(bf16[2,112,128]{2,1,0:T(8,128)(2,1)S(1)} %pad_maximum_fusion.refs_0_), channel_id=1, source_target_pairs={{0,4},{1,5},{2,6},{3,7},{4,0},{5,1},{6,2},{7,3},{8,12},{9,13},{10,... | collective-permute-start | bytes 172040 | tf_op jit(solution)/shard_map/ppermute | solution.py:138
  9.5 1.3 %collective-permute-start.4 = (bf16[2,112,128]{2,1,0:T(8,128)(2,1)S(1)}, bf16[2,112,128]{2,1,0:T(8,128)(2,1)S(1)}, u32[]{:S(2)}, u32[]{:S(2)}) collective-permute-start(bf16[2,112,128]{2,1,0:T(8,128)(2,1)S(1)} %constant_dynamic-update-slice_fusion.refs_1_.refs_2_), channel_id=1, source_target_pairs={{0,4},{1,5},{2,6},{3,7},{4,0},{5,1},{6,2},{7,3},{8,12},{9,13},{10,... | collective-permute-start | bytes 172040 | tf_op jit(solution)/shard_map/ppermute | solution.py:138
  11.3 3.3 %collective-permute-start.6 = (f32[8,416]{1,0:T(8,128)S(1)}, f32[8,416]{1,0:T(8,128)S(1)}, u32[]{:S(2)}, u32[]{:S(2)}) collective-permute-start(f32[8,416]{1,0:T(8,128)S(1)} %shard_map.59), channel_id=1, source_target_pairs={{0,12},{1,13},{2,14},{3,15},{4,8},{5,9},{6,10},{7,11},{8,4},{9,5},... | collective-permute-start | bytes 39944 | tf_op jit(solution)/shard_map/ppermute | solution.py:138

commit v8 on v6

--- a/solution.py
+++ b/solution.py
@@ -11,7 +11,7 @@
 IN_VMEM = pl.BlockSpec(memory_space=VMEM)
 LANES = 128
 CHUNK = 2
-AHEAD = 2
+AHEAD = 3
 
 
 def near(x):
@@ -39,18 +39,16 @@
 
 
 def augmented(block, features, own):
-    x = block.astype(jnp.float32)
-    row = lax.broadcasted_iota(jnp.int32, x.shape, 0)
-    x = jnp.where(row < features, x, 0.0)
+    x = block[:features].astype(jnp.float32)
     half = -0.5 * jnp.sum(x * x, axis=0, keepdims=True)
     high = half.astype(jnp.bfloat16).astype(jnp.float32)
     rest = half - high
     middle = rest.astype(jnp.bfloat16).astype(jnp.float32)
-    parts = [high, middle, rest - middle]
-    rows = [1.0, 1.0, 1.0] + parts if own else parts + [1.0, 1.0, 1.0]
-    for place, value in enumerate(rows):
-        x = jnp.where(row == features + place, value, x)
-    return x.astype(jnp.bfloat16)
+    row = lax.broadcasted_iota(jnp.int32, (8, x.shape[1]), 0)
+    below = jnp.where(row < 6, 1.0, 0.0)
+    for place, value in enumerate([high, middle, rest - middle], 3 if own else 0):
+        below = jnp.where(row == place, value, below)
+    return jnp.concatenate([x, below], axis=0).astype(jnp.bfloat16)
 
 
 def rest_tile(rests, features):

time: 15.4 us -> 15.4 us (level)
  no operation moved by 1% of the time
where the time goes in v8:
time: 15.4 us; the launch traced here: 15.2 us
  starting transfers between devices  8.67 us (56%)
  Pallas kernels  3.82 us (25%)
  waiting for transfers between devices  2.03 us (13%)
  other arithmetic  0.62 us (4%)
    ppermute x2, starting transfers between devices, turn(): return lax.ppermute(x, ('rows', 'cols'), pairs)  4.55 us
    ppermute x5, starting transfers between devices, swap(): return lax.ppermute(x, ('rows', 'cols'), pairs)  4.12 us
    pallas_call x4, Pallas kernels, add(): pl.pallas_call(functools.partial(add_blocks, features, counts), out_shape...  2.83 us
    ppermute x5, waiting for transfers between devices, swap(): return lax.ppermute(x, ('rows', 'cols'), pairs)  1.99 us
    pallas_call x1, Pallas kernels, local(): pl.pallas_call(prepare_kernel, out_shape=(VMEM((height, width), jnp.bfloa...  0.99 us
    add x1, other arithmetic, local(): return total + swap(partial, mesh_shape, 3, 0)  0.61 us
  transfers between devices with their start and end apart: 7, of which 3 were waited for; matrix products, arithmetic and copies ran while one was open for 0% of the time, Pallas kernels for 16%

profile of v8, /device:TPU:0, one launch (start us, length us, event | category | flops | bytes accessed | tf_op | source)
XLA Modules:
  0.0 15.2 jit_solution(13123712274434761994)
XLA Ops:
  0.0 1.0 %shard_map.55 = (bf16[32,416]{1,0:T(8,128)(2,1)S(1)}, f32[8,416]{1,0:T(8,128)S(1)}, bf16[112,128]{1,0:T(8,128)(2,1)S(1)}) custom-call(f32[24,416]{1,0:T(8,128)} %points_ref.1, f32[1,24]{1,0:T(1,128)} %bitcast.10, f32[1,416]{1,0:T(1,128)} %bitcast.8, s32[7,416]{1,0:T(8,128)} %probes_ref.1, f32[1,416]{1,0:T(1,128)} %bitcast.9), custom_call_target="tpu_custom_call" | custom-call | tf_op jit(solution)/shard_map/pallas_call | solution.py:159
  1.0 4.0 %collective-permute-start = (bf16[1,112,128]{2,1,0:T(8,128)(2,1)S(1)}, bf16[1,112,128]{2,1,0:T(8,128)(2,1)S(1)}, u32[]{:S(2)}, u32[]{:S(2)}) collective-permute-start(bf16[1,112,128]{2,1,0:T(8,128)(2,1)S(1)} %bitcast.4), channel_id=1, source_target_pairs={{0,2},{1,3},{2,1},{3,0},{4,6},{5,7},{6,5},{7,4},{8,10},{9,11},{10,... | collective-permute-start | bytes 86024 | tf_op jit(solution)/shard_map/ppermute | solution.py:142
  5.0 0.5 %collective-permute-start.3 = (bf16[1,112,128]{2,1,0:T(8,128)(2,1)S(1)}, bf16[1,112,128]{2,1,0:T(8,128)(2,1)S(1)}, u32[]{:S(2)}, u32[]{:S(2)}) collective-permute-start(bf16[1,112,128]{2,1,0:T(8,128)(2,1)S(1)} %bitcast.5), channel_id=1, source_target_pairs={{0,7},{1,6},{2,4},{3,5},{4,3},{5,2},{6,0},{7,1},{8,15},{9,14},{10,... | collective-permute-start | bytes 86024 | tf_op jit(solution)/shard_map/ppermute | solution.py:142
  5.5 0.2 %collective-permute-start.2 = (bf16[1,112,128]{2,1,0:T(8,128)(2,1)S(1)}, bf16[1,112,128]{2,1,0:T(8,128)(2,1)S(1)}, u32[]{:S(2)}, u32[]{:S(2)}) collective-permute-start(bf16[1,112,128]{2,1,0:T(8,128)(2,1)S(1)} %bitcast.6), channel_id=1, source_target_pairs={{0,5},{1,4},{2,7},{3,6},{4,1},{5,0},{6,3},{7,2},{8,13},{9,12},{10,... | collective-permute-start | bytes 86024 | tf_op jit(solution)/shard_map/ppermute | solution.py:134
  5.8 2.1 %collective-permute-start.5 = (bf16[32,416]{1,0:T(8,128)(2,1)S(1)}, bf16[32,416]{1,0:T(8,128)(2,1)S(1)}, u32[]{:S(2)}, u32[]{:S(2)}) collective-permute-start(bf16[32,416]{1,0:T(8,128)(2,1)S(1)} %get-tuple-element.11.refs_1_.refs_3_), channel_id=1, source_target_pairs={{0,12},{1,13},{2,14},{3,15},{4,8},{5,9},{6,10},{7,11},{8,4},{9,5},... | collective-permute-start | bytes 79880 | tf_op jit(solution)/shard_map/ppermute | solution.py:134
  7.9 0.0 collective-permute-done
  7.9 0.5 %shard_map.56.refs_4_ = f32[8,416]{1,0:T(8,128)S(1)} custom-call(bf16[2,112,128]{2,1,0:T(8,128)(2,1)S(1)} %pad_maximum_fusion.refs_0_, bf16[32,416]{1,0:T(8,128)(2,1)S(1)} %get-tuple-element.11.refs_1_.refs_3_, f32[8,416]{1,0:T(8,128)S(1)} %get-tuple-element.12.refs_2_), custom_call_target="tpu_custom_call" | custom-call | flops 7088373760 | tf_op jit(solution)/shard_map/pallas_call | solution.py:120
  8.4 0.1 collective-permute-start.1
  8.5 1.1 %collective-permute-done.2 = bf16[1,112,128]{2,1,0:T(8,128)(2,1)S(1)} collective-permute-done((bf16[1,112,128]{2,1,0:T(8,128)(2,1)S(1)}, bf16[1,112,128]{2,1,0:T(8,128)(2,1)S(1)}, u32[]{:S(2)}, u32[]{:S(2)}) %collective-permute-start.2) | collective-permute-done | bytes 28704 | tf_op jit(solution)/shard_map/ppermute | solution.py:134
  9.5 0.0 collective-permute-done.3
  9.5 0.2 %collective-permute-start.4 = (bf16[2,112,128]{2,1,0:T(8,128)(2,1)S(1)}, bf16[2,112,128]{2,1,0:T(8,128)(2,1)S(1)}, u32[]{:S(2)}, u32[]{:S(2)}) collective-permute-start(bf16[2,112,128]{2,1,0:T(8,128)(2,1)S(1)} %constant_dynamic-update-slice_fusion.refs_1_.refs_2_), channel_id=1, source_target_pairs={{0,4},{1,5},{2,6},{3,7},{4,0},{5,1},{6,2},{7,3},{8,12},{9,13},{10,... | collective-permute-start | bytes 172040 | tf_op jit(solution)/shard_map/ppermute | solution.py:134
  9.7 0.0 collective-permute-done.5.refs_3_.refs_1_
  9.7 0.0 collective-permute-done.1.refs_0_.refs_1_
  9.7 0.9 %shard_map.58.refs_2_ = f32[8,416]{1,0:T(8,128)S(1)} custom-call(bf16[2,112,128]{2,1,0:T(8,128)(2,1)S(1)} %pad_maximum_fusion.refs_0_, bf16[2,112,128]{2,1,0:T(8,128)(2,1)S(1)} %collective-permute-done.1.refs_0_.refs_1_, bf16[2,112,128]{2,1,0:T(8,128)(2,1)S(1)} %constant_dynamic-update-slice_fusion.refs_1_.refs_2_, ...), custom_call_target="tpu_custom_call" | custom-call | flops 21265121280 | tf_op jit(solution)/shard_map/pallas_call | solution.py:120
  10.7 0.2 %collective-permute-done.4.refs_2_.refs_0_ = bf16[2,112,128]{2,1,0:T(8,128)(2,1)S(1)} collective-permute-done((bf16[2,112,128]{2,1,0:T(8,128)(2,1)S(1)}, bf16[2,112,128]{2,1,0:T(8,128)(2,1)S(1)}, u32[]{:S(2)}, u32[]{:S(2)}) %collective-permute-start.4) | collective-permute-done | bytes 57376 | tf_op jit(solution)/shard_map/ppermute | solution.py:134
  10.8 0.5 %shard_map.59 = f32[8,416]{1,0:T(8,128)S(1)} custom-call(bf16[2,112,128]{2,1,0:T(8,128)(2,1)S(1)} %collective-permute-done.4.refs_2_.refs_0_, bf16[32,416]{1,0:T(8,128)(2,1)S(1)} %collective-permute-done.5.refs_3_.refs_1_, f32[8,416]{1,0:T(8,128)S(1)} %shard_map.58.refs_2_), custom_call_target="tpu_custom_call" | custom-call | flops 7088373760 | tf_op jit(solution)/shard_map/pallas_call | solution.py:120
  11.3 1.6 %collective-permute-start.6 = (f32[8,416]{1,0:T(8,128)S(1)}, f32[8,416]{1,0:T(8,128)S(1)}, u32[]{:S(2)}, u32[]{:S(2)}) collective-permute-start(f32[8,416]{1,0:T(8,128)S(1)} %shard_map.59), channel_id=1, source_target_pairs={{0,12},{1,13},{2,14},{3,15},{4,8},{5,9},{6,10},{7,11},{8,4},{9,5},... | collective-permute-start | bytes 39944 | tf_op jit(solution)/shard_map/ppermute | solution.py:134
  12.9 1.0 %shard_map.57 = f32[8,416]{1,0:T(8,128)S(1)} custom-call(bf16[2,112,128]{2,1,0:T(8,128)(2,1)S(1)} %collective-permute-done.1.refs_0_.refs_1_, bf16[2,112,128]{2,1,0:T(8,128)(2,1)S(1)} %constant_dynamic-update-slice_fusion.refs_1_.refs_2_, bf16[2,112,128]{2,1,0:T(8,128)(2,1)S(1)} %collective-permute-done.4.refs_2_.refs_0_, ...), custom_call_target="tpu_custom_call" | custom-call | flops 21265121280 | tf_op jit(solution)/shard_map/pallas_call | solution.py:120
  13.8 0.8 %collective-permute-done.6 = f32[8,416]{1,0:T(8,128)S(1)} collective-permute-done((f32[8,416]{1,0:T(8,128)S(1)}, f32[8,416]{1,0:T(8,128)S(1)}, u32[]{:S(2)}, u32[]{:S(2)}) %collective-permute-start.6) | collective-permute-done | bytes 13344 | tf_op jit(solution)/shard_map/ppermute | solution.py:134
  14.6 0.6 %add.3 = f32[8,416]{1,0:T(8,128)} add(f32[8,416]{1,0:T(8,128)S(1)} %shard_map.57, f32[8,416]{1,0:T(8,128)S(1)} %collective-permute-done.6) | non-fusion elementwise | flops 3328 | bytes 39936 | tf_op jit(solution)/shard_map/add | solution.py:185
  (3 shorter events, 0.0 us)
Async XLA Ops:
  1.0 6.9 %collective-permute-start = (bf16[1,112,128]{2,1,0:T(8,128)(2,1)S(1)}, bf16[1,112,128]{2,1,0:T(8,128)(2,1)S(1)}, u32[]{:S(2)}, u32[]{:S(2)}) collective-permute-start(bf16[1,112,128]{2,1,0:T(8,128)(2,1)S(1)} %bitcast.4), channel_id=1, source_target_pairs={{0,2},{1,3},{2,1},{3,0},{4,6},{5,7},{6,5},{7,4},{8,10},{9,11},{10,... | collective-permute-start | bytes 86024 | tf_op jit(solution)/shard_map/ppermute | solution.py:142
  5.0 4.5 %collective-permute-start.3 = (bf16[1,112,128]{2,1,0:T(8,128)(2,1)S(1)}, bf16[1,112,128]{2,1,0:T(8,128)(2,1)S(1)}, u32[]{:S(2)}, u32[]{:S(2)}) collective-permute-start(bf16[1,112,128]{2,1,0:T(8,128)(2,1)S(1)} %bitcast.5), channel_id=1, source_target_pairs={{0,7},{1,6},{2,4},{3,5},{4,3},{5,2},{6,0},{7,1},{8,15},{9,14},{10,... | collective-permute-start | bytes 86024 | tf_op jit(solution)/shard_map/ppermute | solution.py:142
  5.5 4.0 %collective-permute-start.2 = (bf16[1,112,128]{2,1,0:T(8,128)(2,1)S(1)}, bf16[1,112,128]{2,1,0:T(8,128)(2,1)S(1)}, u32[]{:S(2)}, u32[]{:S(2)}) collective-permute-start(bf16[1,112,128]{2,1,0:T(8,128)(2,1)S(1)} %bitcast.6), channel_id=1, source_target_pairs={{0,5},{1,4},{2,7},{3,6},{4,1},{5,0},{6,3},{7,2},{8,13},{9,12},{10,... | collective-permute-start | bytes 86024 | tf_op jit(solution)/shard_map/ppermute | solution.py:134
  5.8 3.9 %collective-permute-start.5 = (bf16[32,416]{1,0:T(8,128)(2,1)S(1)}, bf16[32,416]{1,0:T(8,128)(2,1)S(1)}, u32[]{:S(2)}, u32[]{:S(2)}) collective-permute-start(bf16[32,416]{1,0:T(8,128)(2,1)S(1)} %get-tuple-element.11.refs_1_.refs_3_), channel_id=1, source_target_pairs={{0,12},{1,13},{2,14},{3,15},{4,8},{5,9},{6,10},{7,11},{8,4},{9,5},... | collective-permute-start | bytes 79880 | tf_op jit(solution)/shard_map/ppermute | solution.py:134
  8.4 1.4 %collective-permute-start.1 = (bf16[2,112,128]{2,1,0:T(8,128)(2,1)S(1)}, bf16[2,112,128]{2,1,0:T(8,128)(2,1)S(1)}, u32[]{:S(2)}, u32[]{:S(2)}) collective-permute-start(bf16[2,112,128]{2,1,0:T(8,128)(2,1)S(1)} %pad_maximum_fusion.refs_0_), channel_id=1, source_target_pairs={{0,4},{1,5},{2,6},{3,7},{4,0},{5,1},{6,2},{7,3},{8,12},{9,13},{10,... | collective-permute-start | bytes 172040 | tf_op jit(solution)/shard_map/ppermute | solution.py:134
  9.5 1.3 %collective-permute-start.4 = (bf16[2,112,128]{2,1,0:T(8,128)(2,1)S(1)}, bf16[2,112,128]{2,1,0:T(8,128)(2,1)S(1)}, u32[]{:S(2)}, u32[]{:S(2)}) collective-permute-start(bf16[2,112,128]{2,1,0:T(8,128)(2,1)S(1)} %constant_dynamic-update-slice_fusion.refs_1_.refs_2_), channel_id=1, source_target_pairs={{0,4},{1,5},{2,6},{3,7},{4,0},{5,1},{6,2},{7,3},{8,12},{9,13},{10,... | collective-permute-start | bytes 172040 | tf_op jit(solution)/shard_map/ppermute | solution.py:134
  11.3 3.3 %collective-permute-start.6 = (f32[8,416]{1,0:T(8,128)S(1)}, f32[8,416]{1,0:T(8,128)S(1)}, u32[]{:S(2)}, u32[]{:S(2)}) collective-permute-start(f32[8,416]{1,0:T(8,128)S(1)} %shard_map.59), channel_id=1, source_target_pairs={{0,12},{1,13},{2,14},{3,15},{4,8},{5,9},{6,10},{7,11},{8,4},{9,5},... | collective-permute-start | bytes 39944 | tf_op jit(solution)/shard_map/ppermute | solution.py:134

commit v9 on v6

--- a/solution.py
+++ b/solution.py
@@ -136,10 +136,10 @@
     return lax.ppermute(x, ("rows", "cols"), pairs)
 
 
-def turn(x, mesh_shape, row_bits, places):
+def turn(x, mesh_shape, crossed, places):
     rows, cols = mesh_shape
     pairs = [
-        (r * cols + c, (r ^ row_bits) * cols + c // 4 * 4 + places[c % 4]) for r in range(rows) for c in range(cols)
+        (r * cols + c, (r ^ crossed[c % 4]) * cols + c // 4 * 4 + places[c % 4]) for r in range(rows) for c in range(cols)
     ]
     return lax.ppermute(x, ("rows", "cols"), pairs)
 
@@ -172,9 +172,9 @@
     for step in [(1, bits) for bits in powers(cols)[:-2]] + [(bits + 1, 0) for bits in powers(rows)[:-2]]:
         one = jnp.concatenate([one, swap(one, mesh_shape, *step)], axis=0)
     peer = swap(block, mesh_shape, 3, 0)
-    next_to = swap(one, mesh_shape, 1, 1)
-    ahead = turn(one, mesh_shape, 0, (2, 3, 1, 0))
-    behind = turn(one, mesh_shape, 1, (3, 2, 0, 1))
+    next_to = turn(one, mesh_shape, (1, 1, 1, 1), (1, 0, 3, 2))
+    ahead = turn(one, mesh_shape, (0, 0, 1, 0), (2, 3, 1, 0))
+    behind = turn(one, mesh_shape, (1, 1, 1, 1), (3, 2, 0, 1))
     early = jnp.concatenate([one, ahead], axis=0)
     late = jnp.concatenate([next_to, behind], axis=0)
     total = add(features, [early], block, base)

time: 15.4 us -> 15.4 us (level)
    ppermute x2 -> x3, waiting for transfers between devices: 0.04 us -> 1.11 us  [turn(): return lax.ppermute(x, ('rows', 'cols'), pairs)]
    ppermute x5 -> x4, waiting for transfers between devices: 2 us -> 0.93 us  [swap(): return lax.ppermute(x, ('rows', 'cols'), pairs)]
    ppermute x5 -> x4, starting transfers between devices: 4.12 us -> 3.89 us  [swap(): return lax.ppermute(x, ('rows', 'cols'), pairs)]
    ppermute x2 -> x3, starting transfers between devices: 4.55 us -> 4.78 us  [turn(): return lax.ppermute(x, ('rows', 'cols'), pairs)]
where the time goes in v9:
time: 15.4 us; the launch traced here: 15.2 us
  starting transfers between devices  8.67 us (56%)
  Pallas kernels  3.82 us (25%)
  waiting for transfers between devices  2.05 us (13%)
  other arithmetic  0.62 us (4%)
    ppermute x3, starting transfers between devices, turn(): return lax.ppermute(x, ('rows', 'cols'), pairs)  4.78 us
    ppermute x4, starting transfers between devices, swap(): return lax.ppermute(x, ('rows', 'cols'), pairs)  3.89 us
    pallas_call x4, Pallas kernels, add(): pl.pallas_call(functools.partial(add_blocks, features, counts), out_shape...  2.83 us
    ppermute x3, waiting for transfers between devices, turn(): return lax.ppermute(x, ('rows', 'cols'), pairs)  1.11 us
    pallas_call x1, Pallas kernels, local(): pl.pallas_call(prepare_kernel, out_shape=(VMEM((height, width), jnp.bfloa...  0.99 us
    ppermute x4, waiting for transfers between devices, swap(): return lax.ppermute(x, ('rows', 'cols'), pairs)  0.93 us
    add x1, other arithmetic, local(): return total + swap(partial, mesh_shape, 3, 0)  0.61 us
  transfers between devices with their start and end apart: 7, of which 3 were waited for; matrix products, arithmetic and copies ran while one was open for 0% of the time, Pallas kernels for 16%

profile of v9, /device:TPU:0, one launch (start us, length us, event | category | flops | bytes accessed | tf_op | source)
XLA Modules:
  0.0 15.2 jit_solution(13627521294191666682)
XLA Ops:
  0.0 1.0 %shard_map.55 = (bf16[32,416]{1,0:T(8,128)(2,1)S(1)}, f32[8,416]{1,0:T(8,128)S(1)}, bf16[112,128]{1,0:T(8,128)(2,1)S(1)}) custom-call(f32[24,416]{1,0:T(8,128)} %points_ref.1, f32[1,24]{1,0:T(1,128)} %bitcast.10, f32[1,416]{1,0:T(1,128)} %bitcast.8, s32[7,416]{1,0:T(8,128)} %probes_ref.1, f32[1,416]{1,0:T(1,128)} %bitcast.9), custom_call_target="tpu_custom_call" | custom-call | tf_op jit(solution)/shard_map/pallas_call | solution.py:161
  1.0 4.0 %collective-permute-start = (bf16[1,112,128]{2,1,0:T(8,128)(2,1)S(1)}, bf16[1,112,128]{2,1,0:T(8,128)(2,1)S(1)}, u32[]{:S(2)}, u32[]{:S(2)}) collective-permute-start(bf16[1,112,128]{2,1,0:T(8,128)(2,1)S(1)} %bitcast.4), channel_id=1, source_target_pairs={{0,2},{1,3},{2,5},{3,0},{4,6},{5,7},{6,1},{7,4},{8,10},{9,11},{10,... | collective-permute-start | bytes 86024 | tf_op jit(solution)/shard_map/ppermute | solution.py:144
  5.0 0.5 %collective-permute-start.3 = (bf16[1,112,128]{2,1,0:T(8,128)(2,1)S(1)}, bf16[1,112,128]{2,1,0:T(8,128)(2,1)S(1)}, u32[]{:S(2)}, u32[]{:S(2)}) collective-permute-start(bf16[1,112,128]{2,1,0:T(8,128)(2,1)S(1)} %bitcast.5), channel_id=1, source_target_pairs={{0,7},{1,6},{2,4},{3,5},{4,3},{5,2},{6,0},{7,1},{8,15},{9,14},{10,... | collective-permute-start | bytes 86024 | tf_op jit(solution)/shard_map/ppermute | solution.py:144
  5.6 0.2 %collective-permute-start.2 = (bf16[1,112,128]{2,1,0:T(8,128)(2,1)S(1)}, bf16[1,112,128]{2,1,0:T(8,128)(2,1)S(1)}, u32[]{:S(2)}, u32[]{:S(2)}) collective-permute-start(bf16[1,112,128]{2,1,0:T(8,128)(2,1)S(1)} %bitcast.6), channel_id=1, source_target_pairs={{0,5},{1,4},{2,7},{3,6},{4,1},{5,0},{6,3},{7,2},{8,13},{9,12},{10,... | collective-permute-start | bytes 86024 | tf_op jit(solution)/shard_map/ppermute | solution.py:144
  5.8 2.1 %collective-permute-start.5 = (bf16[32,416]{1,0:T(8,128)(2,1)S(1)}, bf16[32,416]{1,0:T(8,128)(2,1)S(1)}, u32[]{:S(2)}, u32[]{:S(2)}) collective-permute-start(bf16[32,416]{1,0:T(8,128)(2,1)S(1)} %get-tuple-element.11.refs_1_.refs_3_), channel_id=1, source_target_pairs={{0,12},{1,13},{2,14},{3,15},{4,8},{5,9},{6,10},{7,11},{8,4},{9,5},... | collective-permute-start | bytes 79880 | tf_op jit(solution)/shard_map/ppermute | solution.py:136
  7.9 0.0 collective-permute-done
  7.9 0.5 %shard_map.56.refs_4_ = f32[8,416]{1,0:T(8,128)S(1)} custom-call(bf16[2,112,128]{2,1,0:T(8,128)(2,1)S(1)} %pad_maximum_fusion.refs_0_, bf16[32,416]{1,0:T(8,128)(2,1)S(1)} %get-tuple-element.11.refs_1_.refs_3_, f32[8,416]{1,0:T(8,128)S(1)} %get-tuple-element.12.refs_2_), custom_call_target="tpu_custom_call" | custom-call | flops 7088373760 | tf_op jit(solution)/shard_map/pallas_call | solution.py:122
  8.4 0.1 collective-permute-start.1
  8.5 1.1 %collective-permute-done.2 = bf16[1,112,128]{2,1,0:T(8,128)(2,1)S(1)} collective-permute-done((bf16[1,112,128]{2,1,0:T(8,128)(2,1)S(1)}, bf16[1,112,128]{2,1,0:T(8,128)(2,1)S(1)}, u32[]{:S(2)}, u32[]{:S(2)}) %collective-permute-start.2) | collective-permute-done | bytes 28704 | tf_op jit(solution)/shard_map/ppermute | solution.py:144
  9.5 0.0 collective-permute-done.3
  9.5 0.2 %collective-permute-start.4 = (bf16[2,112,128]{2,1,0:T(8,128)(2,1)S(1)}, bf16[2,112,128]{2,1,0:T(8,128)(2,1)S(1)}, u32[]{:S(2)}, u32[]{:S(2)}) collective-permute-start(bf16[2,112,128]{2,1,0:T(8,128)(2,1)S(1)} %constant_dynamic-update-slice_fusion.refs_1_.refs_2_), channel_id=1, source_target_pairs={{0,4},{1,5},{2,6},{3,7},{4,0},{5,1},{6,2},{7,3},{8,12},{9,13},{10,... | collective-permute-start | bytes 172040 | tf_op jit(solution)/shard_map/ppermute | solution.py:136
  9.7 0.0 collective-permute-done.5.refs_3_.refs_1_
  9.7 0.0 collective-permute-done.1.refs_0_.refs_1_
  9.7 0.9 %shard_map.58.refs_2_ = f32[8,416]{1,0:T(8,128)S(1)} custom-call(bf16[2,112,128]{2,1,0:T(8,128)(2,1)S(1)} %pad_maximum_fusion.refs_0_, bf16[2,112,128]{2,1,0:T(8,128)(2,1)S(1)} %collective-permute-done.1.refs_0_.refs_1_, bf16[2,112,128]{2,1,0:T(8,128)(2,1)S(1)} %constant_dynamic-update-slice_fusion.refs_1_.refs_2_, ...), custom_call_target="tpu_custom_call" | custom-call | flops 21265121280 | tf_op jit(solution)/shard_map/pallas_call | solution.py:122
  10.7 0.2 %collective-permute-done.4.refs_2_.refs_0_ = bf16[2,112,128]{2,1,0:T(8,128)(2,1)S(1)} collective-permute-done((bf16[2,112,128]{2,1,0:T(8,128)(2,1)S(1)}, bf16[2,112,128]{2,1,0:T(8,128)(2,1)S(1)}, u32[]{:S(2)}, u32[]{:S(2)}) %collective-permute-start.4) | collective-permute-done | bytes 57376 | tf_op jit(solution)/shard_map/ppermute | solution.py:136
  10.9 0.5 %shard_map.59 = f32[8,416]{1,0:T(8,128)S(1)} custom-call(bf16[2,112,128]{2,1,0:T(8,128)(2,1)S(1)} %collective-permute-done.4.refs_2_.refs_0_, bf16[32,416]{1,0:T(8,128)(2,1)S(1)} %collective-permute-done.5.refs_3_.refs_1_, f32[8,416]{1,0:T(8,128)S(1)} %shard_map.58.refs_2_), custom_call_target="tpu_custom_call" | custom-call | flops 7088373760 | tf_op jit(solution)/shard_map/pallas_call | solution.py:122
  11.3 1.6 %collective-permute-start.6 = (f32[8,416]{1,0:T(8,128)S(1)}, f32[8,416]{1,0:T(8,128)S(1)}, u32[]{:S(2)}, u32[]{:S(2)}) collective-permute-start(f32[8,416]{1,0:T(8,128)S(1)} %shard_map.59), channel_id=1, source_target_pairs={{0,12},{1,13},{2,14},{3,15},{4,8},{5,9},{6,10},{7,11},{8,4},{9,5},... | collective-permute-start | bytes 39944 | tf_op jit(solution)/shard_map/ppermute | solution.py:136
  12.9 0.9 %shard_map.57 = f32[8,416]{1,0:T(8,128)S(1)} custom-call(bf16[2,112,128]{2,1,0:T(8,128)(2,1)S(1)} %collective-permute-done.1.refs_0_.refs_1_, bf16[2,112,128]{2,1,0:T(8,128)(2,1)S(1)} %constant_dynamic-update-slice_fusion.refs_1_.refs_2_, bf16[2,112,128]{2,1,0:T(8,128)(2,1)S(1)} %collective-permute-done.4.refs_2_.refs_0_, ...), custom_call_target="tpu_custom_call" | custom-call | flops 21265121280 | tf_op jit(solution)/shard_map/pallas_call | solution.py:122
  13.8 0.8 %collective-permute-done.6 = f32[8,416]{1,0:T(8,128)S(1)} collective-permute-done((f32[8,416]{1,0:T(8,128)S(1)}, f32[8,416]{1,0:T(8,128)S(1)}, u32[]{:S(2)}, u32[]{:S(2)}) %collective-permute-start.6) | collective-permute-done | bytes 13344 | tf_op jit(solution)/shard_map/ppermute | solution.py:136
  14.6 0.6 %add.3 = f32[8,416]{1,0:T(8,128)} add(f32[8,416]{1,0:T(8,128)S(1)} %shard_map.57, f32[8,416]{1,0:T(8,128)S(1)} %collective-permute-done.6) | non-fusion elementwise | flops 3328 | bytes 39936 | tf_op jit(solution)/shard_map/add | solution.py:187
  (3 shorter events, 0.0 us)
Async XLA Ops:
  1.0 6.9 %collective-permute-start = (bf16[1,112,128]{2,1,0:T(8,128)(2,1)S(1)}, bf16[1,112,128]{2,1,0:T(8,128)(2,1)S(1)}, u32[]{:S(2)}, u32[]{:S(2)}) collective-permute-start(bf16[1,112,128]{2,1,0:T(8,128)(2,1)S(1)} %bitcast.4), channel_id=1, source_target_pairs={{0,2},{1,3},{2,5},{3,0},{4,6},{5,7},{6,1},{7,4},{8,10},{9,11},{10,... | collective-permute-start | bytes 86024 | tf_op jit(solution)/shard_map/ppermute | solution.py:144
  5.0 4.5 %collective-permute-start.3 = (bf16[1,112,128]{2,1,0:T(8,128)(2,1)S(1)}, bf16[1,112,128]{2,1,0:T(8,128)(2,1)S(1)}, u32[]{:S(2)}, u32[]{:S(2)}) collective-permute-start(bf16[1,112,128]{2,1,0:T(8,128)(2,1)S(1)} %bitcast.5), channel_id=1, source_target_pairs={{0,7},{1,6},{2,4},{3,5},{4,3},{5,2},{6,0},{7,1},{8,15},{9,14},{10,... | collective-permute-start | bytes 86024 | tf_op jit(solution)/shard_map/ppermute | solution.py:144
  5.6 4.0 %collective-permute-start.2 = (bf16[1,112,128]{2,1,0:T(8,128)(2,1)S(1)}, bf16[1,112,128]{2,1,0:T(8,128)(2,1)S(1)}, u32[]{:S(2)}, u32[]{:S(2)}) collective-permute-start(bf16[1,112,128]{2,1,0:T(8,128)(2,1)S(1)} %bitcast.6), channel_id=1, source_target_pairs={{0,5},{1,4},{2,7},{3,6},{4,1},{5,0},{6,3},{7,2},{8,13},{9,12},{10,... | collective-permute-start | bytes 86024 | tf_op jit(solution)/shard_map/ppermute | solution.py:144
  5.8 4.0 %collective-permute-start.5 = (bf16[32,416]{1,0:T(8,128)(2,1)S(1)}, bf16[32,416]{1,0:T(8,128)(2,1)S(1)}, u32[]{:S(2)}, u32[]{:S(2)}) collective-permute-start(bf16[32,416]{1,0:T(8,128)(2,1)S(1)} %get-tuple-element.11.refs_1_.refs_3_), channel_id=1, source_target_pairs={{0,12},{1,13},{2,14},{3,15},{4,8},{5,9},{6,10},{7,11},{8,4},{9,5},... | collective-permute-start | bytes 79880 | tf_op jit(solution)/shard_map/ppermute | solution.py:136
  8.4 1.4 %collective-permute-start.1 = (bf16[2,112,128]{2,1,0:T(8,128)(2,1)S(1)}, bf16[2,112,128]{2,1,0:T(8,128)(2,1)S(1)}, u32[]{:S(2)}, u32[]{:S(2)}) collective-permute-start(bf16[2,112,128]{2,1,0:T(8,128)(2,1)S(1)} %pad_maximum_fusion.refs_0_), channel_id=1, source_target_pairs={{0,4},{1,5},{2,6},{3,7},{4,0},{5,1},{6,2},{7,3},{8,12},{9,13},{10,... | collective-permute-start | bytes 172040 | tf_op jit(solution)/shard_map/ppermute | solution.py:136
  9.5 1.3 %collective-permute-start.4 = (bf16[2,112,128]{2,1,0:T(8,128)(2,1)S(1)}, bf16[2,112,128]{2,1,0:T(8,128)(2,1)S(1)}, u32[]{:S(2)}, u32[]{:S(2)}) collective-permute-start(bf16[2,112,128]{2,1,0:T(8,128)(2,1)S(1)} %constant_dynamic-update-slice_fusion.refs_1_.refs_2_), channel_id=1, source_target_pairs={{0,4},{1,5},{2,6},{3,7},{4,0},{5,1},{6,2},{7,3},{8,12},{9,13},{10,... | collective-permute-start | bytes 172040 | tf_op jit(solution)/shard_map/ppermute | solution.py:136
  11.3 3.3 %collective-permute-start.6 = (f32[8,416]{1,0:T(8,128)S(1)}, f32[8,416]{1,0:T(8,128)S(1)}, u32[]{:S(2)}, u32[]{:S(2)}) collective-permute-start(f32[8,416]{1,0:T(8,128)S(1)} %shard_map.59), channel_id=1, source_target_pairs={{0,12},{1,13},{2,14},{3,15},{4,8},{5,9},{6,10},{7,11},{8,4},{9,5},... | collective-permute-start | bytes 39944 | tf_op jit(solution)/shard_map/ppermute | solution.py:136
